TPU v7x, 512 devices: a whole 4x4x16 slice. The times are simulated.
512 devices in a mesh: gx: 4 (over y), gy: 16 (over z), gz: 8 (over x, core).
Axes of the slice: x: 4, y: 4, z: 16, core: 2. Of those that a mesh axis runs over, the one named last changes fastest.
Arguments:
- state: float32 [3, 128, 640, 512], P(None, 'gz', 'gy', 'gx'), may hold values from -6 to 6
- right_side: float32 [3, 128, 640, 512], P(None, 'gz', 'gy', 'gx'), may hold values from -6 to 6
- permeability: bfloat16 [128, 640, 512], P('gz', 'gy', 'gx'), may hold values from 0.099609375 to 10
- pore_volume: bfloat16 [128, 640, 512], P('gz', 'gy', 'gx'), may hold values from 0.019897461 to 0.19921875
- facies: int32 [128], P('gz'), may hold values from 0 to 3
- storage_table: float32 [4, 3, 3], replicated, may hold values from -0.3 to 2, as said below
- coupling_table: float32 [4, 3, 3], replicated, may hold values from -0.3 to 2, as said below
Outputs:
- new_state: float32 [3, 128, 640, 512], P(None, 'gz', 'gy', 'gx')
- correction: float32 [640, 512], P('gy', 'gx')
Inputs may be any that keep to these rules, and one draw needn't show every extreme that they name: `storage_table`: each facies block has a diagonal of 1 to 2 and off-diagonal entries of magnitude at most 0.3. `coupling_table`: each facies block has a diagonal of 1 to 2 and off-diagonal entries of magnitude at most 0.3.
All inputs are finite; a program needn't handle non-finite values.
Results may differ from a plain program's by a relative error of at most 0.0003.
Values sent between devices are 32-bit elements; how exact they have to be, the bound alone decides.
No kernel may reach another device: no remote copies, remote signals or barrier semaphores. Data moves between devices by JAX's collectives and lax.ppermute only.
A program may use at most 64 MiB of HBM per device.

v0:
```python
import jax
import jax.numpy as jnp
from jax import lax
from jax.sharding import PartitionSpec as P

SWEEPS = 8
relax = 0.8


def extended(cells, sides, width):
    for axis, dim in sides:
        count = lax.axis_size(axis)
        ends = count - 1
        head = lax.slice_in_dim(cells, 0, width, axis=dim)
        tail = lax.slice_in_dim(cells, cells.shape[dim] - width, cells.shape[dim], axis=dim)
        cells = jnp.concatenate(
            [
                lax.ppermute(tail, axis, [(i, (i + 1) % count) for i in range(ends)]),
                cells,
                lax.ppermute(head, axis, [((i + 1) % count, i) for i in range(ends)]),
            ],
            axis=dim,
        )
    return cells


def layer_tables(facies, table):
    onehot = (facies[:, None] == jnp.arange(table.shape[0])[None, :]).astype(jnp.float32)
    return jnp.dot(onehot, table.reshape(table.shape[0], 9), precision=lax.Precision.HIGHEST)


def layer_coefficient(rows, row_index, column_index):
    return rows[:, 3 * row_index + column_index][:, None, None]


def neighbours(padded):
    return [
        padded[..., 2:, 1:-1, 1:-1],
        padded[..., :-2, 1:-1, 1:-1],
        padded[..., 1:-1, 2:, 1:-1],
        padded[..., 1:-1, :-2, 1:-1],
        padded[..., 1:-1, 1:-1, 2:],
        padded[..., 1:-1, 1:-1, :-2],
    ]


def face_weights(padded_perm):
    center = padded_perm[1:-1, 1:-1, 1:-1]
    return [2.0 * center * nearby / (center + nearby) for nearby in neighbours(padded_perm)]


def apply_operator(padded_state, weights, storage, storage_rows, coupling_rows):
    center = padded_state[:, 1:-1, 1:-1, 1:-1]
    fluxes = jnp.zeros_like(center)
    for weight, nearby in zip(weights, neighbours(padded_state)):
        fluxes = fluxes + weight[None] * (center - nearby)
    outputs = []
    for row_index in range(3):
        local = sum((layer_coefficient(storage_rows, row_index, k) * center[k] for k in range(3)))
        moved = sum((layer_coefficient(coupling_rows, row_index, k) * fluxes[k] for k in range(3)))
        outputs.append(storage * local + moved)
    return jnp.stack(outputs)


def coarse_planes(residual, weights, storage, storage_rows, coupling_rows):
    first_coupling = layer_coefficient(coupling_rows, 0, 0)
    first_storage = layer_coefficient(storage_rows, 0, 0)
    items = [residual[0], storage * first_storage] + [
        weights[k] * first_coupling for k in range(2, 6)
    ]
    return jnp.stack([jnp.sum(item, axis=0) for item in items])


def jacobi(field, bordered, planes):
    diagonal = planes[1] + planes[2] + planes[3] + planes[4] + planes[5]
    nearby = (
        planes[2] * bordered[2:, 1:-1]
        + planes[3] * bordered[:-2, 1:-1]
        + planes[4] * bordered[1:-1, 2:]
        + planes[5] * bordered[1:-1, :-2]
    )
    return field + relax * (planes[0] - diagonal * field + nearby) / diagonal


def block_solve(weights, storage, storage_rows, coupling_rows, residual):
    face_total = weights[0] + weights[1] + weights[2] + weights[3] + weights[4] + weights[5]
    entries = [
        [
            storage * layer_coefficient(storage_rows, r, c)
            + face_total * layer_coefficient(coupling_rows, r, c)
            for c in range(3)
        ]
        for r in range(3)
    ]

    def cofactor(r, c):
        return (
            entries[(r + 1) % 3][(c + 1) % 3] * entries[(r + 2) % 3][(c + 2) % 3]
            - entries[(r + 1) % 3][(c + 2) % 3] * entries[(r + 2) % 3][(c + 1) % 3]
        )

    factors = [[cofactor(r, c) for c in range(3)] for r in range(3)]
    determinant = (
        entries[0][0] * factors[0][0]
        + entries[0][1] * factors[0][1]
        + entries[0][2] * factors[0][2]
    )
    return jnp.stack(
        [
            (
                factors[0][r] * residual[0]
                + factors[1][r] * residual[1]
                + factors[2][r] * residual[2]
            )
            / determinant
            for r in range(3)
        ]
    )


def per_device(state, right_side, permeability, pore_volume, facies, storage_table, coupling_table):
    perm_wide = permeability.astype(jnp.float32)
    storage = pore_volume.astype(jnp.float32)
    storage_rows = layer_tables(facies, storage_table)
    coupling_rows = layer_tables(facies, coupling_table)
    stacked = jnp.concatenate([state, perm_wide[None]], axis=0)
    padded = extended(stacked, (("gz", 1), ("gy", 2), ("gx", 3)), 1)
    weights = face_weights(padded[3])
    residual = right_side - apply_operator(
        padded[:3], weights, storage, storage_rows, coupling_rows
    )
    planes = coarse_planes(residual, weights, storage, storage_rows, coupling_rows)
    totals = lax.psum(planes, "gz")
    correction = jnp.zeros(totals.shape[1:], jnp.float32)
    for repeat_index in range(SWEEPS):
        bordered = extended(correction, (("gy", 0), ("gx", 1)), 1)
        correction = jacobi(correction, bordered, totals)
    state_one = state.at[0].add(correction[None])
    padded_again = extended(state_one, (("gz", 1), ("gy", 2), ("gx", 3)), 1)
    later_residual = right_side - apply_operator(
        padded_again, weights, storage, storage_rows, coupling_rows
    )
    new_state = state_one + block_solve(
        weights, storage, storage_rows, coupling_rows, later_residual
    )
    return (new_state, correction)


def solution(mesh):
    return jax.shard_map(
        per_device,
        mesh=mesh,
        in_specs=(
            P(None, "gz", "gy", "gx"),
            P(None, "gz", "gy", "gx"),
            P("gz", "gy", "gx"),
            P("gz", "gy", "gx"),
            P("gz"),
            P(),
            P(),
        ),
        out_specs=(P(None, "gz", "gy", "gx"), P("gy", "gx")),
        check_vma=False,
    )
```

profile of v0, /device:TPU:154, one launch (start us, length us, event | category | flops | bytes accessed | tf_op | source)
XLA Modules:
  0.0 306.7 jit_solution(5272867238131126008)
XLA Ops:
  7.3 2.1 collective-permute-start.6
  9.4 3.8 %collective-permute-start.7 = (f32[1,128]{1,0:T(1,128)S(1)}, f32[1,128]{1,0:T(1,128)S(1)}, u32[]{:S(2)}, u32[]{:S(2)}) collective-permute-start(f32[1,128]{1,0:T(1,128)S(1)} %broadcast.56), channel_id=1, source_target_pairs={{0,8},{8,16},{16,24},{24,32},{32,40},{40,48},{48,56},{56,64},{64,7... | collective-permute-start | bytes 1544 | tf_op jit(solution)/shard_map/ppermute | solution.py:18
  15.1 1.9 collective-permute-start
  17.0 3.6 %collective-permute-start.1 = (f32[4,1,40,128]{3,2,1,0:T(8,128)S(1)}, f32[4,1,40,128]{3,2,1,0:T(8,128)S(1)}, u32[]{:S(2)}, u32[]{:S(2)}) collective-permute-start(f32[4,1,40,128]{3,2,1,0:T(8,128)S(1)} %get-tuple-element.39), channel_id=1, source_target_pairs={{1,0},{2,1},{3,2},{4,3},{5,4},{6,5},{7,6},{9,8},{10,9},{11,10},{12... | collective-permute-start | bytes 245768 | tf_op jit(solution)/shard_map/ppermute | solution.py:20
  22.8 3.8 %collective-permute-start.2 = (f32[4,18,1,128]{3,0,2,1:T(4,128)S(1)}, f32[4,18,1,128]{3,0,2,1:T(4,128)S(1)}, u32[]{:S(2)}, u32[]{:S(2)}) collective-permute-start(f32[4,18,1,128]{3,0,2,1:T(4,128)S(1)} %copy.276), channel_id=1, source_target_pairs={{0,8},{8,16},{16,24},{24,32},{32,40},{40,48},{48,56},{56,64},{64,7... | collective-permute-start | bytes 110600 | tf_op jit(solution)/shard_map/ppermute | solution.py:18
  26.6 3.2 %collective-permute-start.3 = (f32[4,18,1,128]{3,0,2,1:T(4,128)S(1)}, f32[4,18,1,128]{3,0,2,1:T(4,128)S(1)}, u32[]{:S(2)}, u32[]{:S(2)}) collective-permute-start(f32[4,18,1,128]{3,0,2,1:T(4,128)S(1)} %copy.277), channel_id=1, source_target_pairs={{8,0},{16,8},{24,16},{32,24},{40,32},{48,40},{56,48},{64,56},{72,6... | collective-permute-start | bytes 110600 | tf_op jit(solution)/shard_map/ppermute | solution.py:20
  34.5 2.2 copy.246
  38.7 4.5 %collective-permute-start.5 = (f32[4,18,42,1]{2,0,3,1:T(4,128)S(1)}, f32[4,18,42,1]{2,0,3,1:T(4,128)S(1)}, u32[]{:S(2)}, u32[]{:S(2)}) collective-permute-start(f32[4,18,42,1]{2,0,3,1:T(4,128)S(1)} %copy.247), channel_id=1, source_target_pairs={{128,0},{256,128},{384,256},{129,1},{257,129},{385,257},{130,2},{2... | collective-permute-start | bytes 36296 | tf_op jit(solution)/shard_map/ppermute | solution.py:20
  49.8 3.3 %fusion.19 = f32[3,16,40,128]{3,2,1,0:T(8,128)S(1)} fusion(f32[3,16,40,128]{3,2,1,0:T(8,128)S(1)} %copy-done, f32[4,18,42,1]{3,2,1,0:T(8,128)S(1)} %copy.248, f32[4,18,1,128]{3,2,1,0:T(1,128)S(1)} %copy.245, f32[4,18,1,128]{3,2,1,0:T(1,128)S(1)} %copy.244, f32[4,1,40,128]{3,2,1,0:T(8,128)S(1)} %collective-permute-done.1, ...), kind=kLoop, calls=%fused_computation.57 | loop fusion | flops 10076160 | bytes 4521600 | tf_op jit(solution)/shard_map/add | solution.py:56
  57.4 4.2 %collective-permute-start.8 = (f32[42,1]{1,0:T(8,128)S(1)}, f32[42,1]{1,0:T(8,128)S(1)}, u32[]{:S(2)}, u32[]{:S(2)}) collective-permute-start(f32[42,1]{1,0:T(8,128)S(1)} %get-tuple-element.70), channel_id=1, source_target_pairs={{128,0},{256,128},{384,256},{129,1},{257,129},{385,257},{130,2},{2... | collective-permute-start | bytes 512 | tf_op jit(solution)/shard_map/ppermute | solution.py:20
  63.1 4.2 %collective-permute-done.9 = f32[42,1]{1,0:T(8,128)S(1)} collective-permute-done((f32[42,1]{1,0:T(8,128)S(1)}, f32[42,1]{1,0:T(8,128)S(1)}, u32[]{:S(2)}, u32[]{:S(2)}) %collective-permute-start.9) | collective-permute-done | bytes 200 | tf_op jit(solution)/shard_map/ppermute | solution.py:18
  67.3 67.1 %all-reduce.4.cloned.1.call-done = f32[6,40,128]{2,1,0:T(8,128)} async-done(((f32[6,40,128]{2,1,0:T(8,128)}), f32[6,40,128]{2,1,0:T(8,128)}) %all-reduce.4.cloned.1.call-update) | async-done | bytes 122896 | tf_op jit(solution)/shard_map/psum | solution.py:133
  135.4 2.4 collective-permute-start.10
  137.8 3.5 %collective-permute-start.11 = (f32[1,128]{1,0:T(1,128)S(1)}, f32[1,128]{1,0:T(1,128)S(1)}, u32[]{:S(2)}, u32[]{:S(2)}) collective-permute-start(f32[1,128]{1,0:T(1,128)S(1)} %get-tuple-element.84), channel_id=1, source_target_pairs={{0,8},{8,16},{16,24},{24,32},{32,40},{40,48},{48,56},{56,64},{64,7... | collective-permute-start | bytes 1544 | tf_op jit(solution)/shard_map/ppermute | solution.py:18
  141.3 3.2 %collective-permute-done.11 = f32[1,128]{1,0:T(1,128)S(1)} collective-permute-done((f32[1,128]{1,0:T(1,128)S(1)}, f32[1,128]{1,0:T(1,128)S(1)}, u32[]{:S(2)}, u32[]{:S(2)}) %collective-permute-start.11) | collective-permute-done | bytes 544 | tf_op jit(solution)/shard_map/ppermute | solution.py:18
  144.5 2.7 collective-permute-start.12
  148.7 4.2 %collective-permute-done.13 = f32[42,1]{1,0:T(8,128)S(1)} collective-permute-done((f32[42,1]{1,0:T(8,128)S(1)}, f32[42,1]{1,0:T(8,128)S(1)}, u32[]{:S(2)}, u32[]{:S(2)}) %collective-permute-start.13) | collective-permute-done | bytes 200 | tf_op jit(solution)/shard_map/ppermute | solution.py:18
  155.8 3.9 %collective-permute-start.15 = (f32[1,128]{1,0:T(1,128)S(1)}, f32[1,128]{1,0:T(1,128)S(1)}, u32[]{:S(2)}, u32[]{:S(2)}) collective-permute-start(f32[1,128]{1,0:T(1,128)S(1)} %get-tuple-element.82), channel_id=1, source_target_pairs={{0,8},{8,16},{16,24},{24,32},{32,40},{40,48},{48,56},{56,64},{64,7... | collective-permute-start | bytes 1544 | tf_op jit(solution)/shard_map/ppermute | solution.py:18
  159.8 2.7 collective-permute-done.15
  162.5 2.4 collective-permute-start.16
  166.5 4.2 %collective-permute-done.17 = f32[42,1]{1,0:T(8,128)S(1)} collective-permute-done((f32[42,1]{1,0:T(8,128)S(1)}, f32[42,1]{1,0:T(8,128)S(1)}, u32[]{:S(2)}, u32[]{:S(2)}) %collective-permute-start.17) | collective-permute-done | bytes 200 | tf_op jit(solution)/shard_map/ppermute | solution.py:18
  173.6 3.9 %collective-permute-start.19 = (f32[1,128]{1,0:T(1,128)S(1)}, f32[1,128]{1,0:T(1,128)S(1)}, u32[]{:S(2)}, u32[]{:S(2)}) collective-permute-start(f32[1,128]{1,0:T(1,128)S(1)} %get-tuple-element.80), channel_id=1, source_target_pairs={{0,8},{8,16},{16,24},{24,32},{32,40},{40,48},{48,56},{56,64},{64,7... | collective-permute-start | bytes 1544 | tf_op jit(solution)/shard_map/ppermute | solution.py:18
  177.5 2.7 collective-permute-done.19
  180.3 2.4 collective-permute-start.20
  184.2 4.2 %collective-permute-done.21 = f32[42,1]{1,0:T(8,128)S(1)} collective-permute-done((f32[42,1]{1,0:T(8,128)S(1)}, f32[42,1]{1,0:T(8,128)S(1)}, u32[]{:S(2)}, u32[]{:S(2)}) %collective-permute-start.21) | collective-permute-done | bytes 200 | tf_op jit(solution)/shard_map/ppermute | solution.py:18
  189.4 2.1 collective-permute-start.22
  191.5 3.9 %collective-permute-start.23 = (f32[1,128]{1,0:T(1,128)S(1)}, f32[1,128]{1,0:T(1,128)S(1)}, u32[]{:S(2)}, u32[]{:S(2)}) collective-permute-start(f32[1,128]{1,0:T(1,128)S(1)} %get-tuple-element.78), channel_id=1, source_target_pairs={{0,8},{8,16},{16,24},{24,32},{32,40},{40,48},{48,56},{56,64},{64,7... | collective-permute-start | bytes 1544 | tf_op jit(solution)/shard_map/ppermute | solution.py:18
  195.4 2.7 collective-permute-done.23
  201.6 4.2 %collective-permute-done.25 = f32[42,1]{1,0:T(8,128)S(1)} collective-permute-done((f32[42,1]{1,0:T(8,128)S(1)}, f32[42,1]{1,0:T(8,128)S(1)}, u32[]{:S(2)}, u32[]{:S(2)}) %collective-permute-start.25) | collective-permute-done | bytes 200 | tf_op jit(solution)/shard_map/ppermute | solution.py:18
  208.7 3.9 %collective-permute-start.27 = (f32[1,128]{1,0:T(1,128)S(1)}, f32[1,128]{1,0:T(1,128)S(1)}, u32[]{:S(2)}, u32[]{:S(2)}) collective-permute-start(f32[1,128]{1,0:T(1,128)S(1)} %get-tuple-element.76), channel_id=1, source_target_pairs={{0,8},{8,16},{16,24},{24,32},{32,40},{40,48},{48,56},{56,64},{64,7... | collective-permute-start | bytes 1544 | tf_op jit(solution)/shard_map/ppermute | solution.py:18
  212.6 2.7 collective-permute-done.27
  218.8 4.2 %collective-permute-done.29 = f32[42,1]{1,0:T(8,128)S(1)} collective-permute-done((f32[42,1]{1,0:T(8,128)S(1)}, f32[42,1]{1,0:T(8,128)S(1)}, u32[]{:S(2)}, u32[]{:S(2)}) %collective-permute-start.29) | collective-permute-done | bytes 200 | tf_op jit(solution)/shard_map/ppermute | solution.py:18
  223.2 1.9 collective-permute-start.30
  225.1 3.9 %collective-permute-start.31 = (f32[1,128]{1,0:T(1,128)S(1)}, f32[1,128]{1,0:T(1,128)S(1)}, u32[]{:S(2)}, u32[]{:S(2)}) collective-permute-start(f32[1,128]{1,0:T(1,128)S(1)} %get-tuple-element.74), channel_id=1, source_target_pairs={{0,8},{8,16},{16,24},{24,32},{32,40},{40,48},{48,56},{56,64},{64,7... | collective-permute-start | bytes 1544 | tf_op jit(solution)/shard_map/ppermute | solution.py:18
  229.0 2.7 collective-permute-done.31
  231.8 1.9 collective-permute-start.32
  235.3 4.2 %collective-permute-done.33 = f32[42,1]{1,0:T(8,128)S(1)} collective-permute-done((f32[42,1]{1,0:T(8,128)S(1)}, f32[42,1]{1,0:T(8,128)S(1)}, u32[]{:S(2)}, u32[]{:S(2)}) %collective-permute-start.33) | collective-permute-done | bytes 200 | tf_op jit(solution)/shard_map/ppermute | solution.py:18
  241.5 3.9 %collective-permute-start.35 = (f32[1,128]{1,0:T(1,128)S(1)}, f32[1,128]{1,0:T(1,128)S(1)}, u32[]{:S(2)}, u32[]{:S(2)}) collective-permute-start(f32[1,128]{1,0:T(1,128)S(1)} %get-tuple-element.72), channel_id=1, source_target_pairs={{0,8},{8,16},{16,24},{24,32},{32,40},{40,48},{48,56},{56,64},{64,7... | collective-permute-start | bytes 1544 | tf_op jit(solution)/shard_map/ppermute | solution.py:18
  245.5 2.7 collective-permute-done.35
  248.2 2.1 collective-permute-start.36
  251.8 4.2 %collective-permute-done.37 = f32[42,1]{1,0:T(8,128)S(1)} collective-permute-done((f32[42,1]{1,0:T(8,128)S(1)}, f32[42,1]{1,0:T(8,128)S(1)}, u32[]{:S(2)}, u32[]{:S(2)}) %collective-permute-start.37) | collective-permute-done | bytes 200 | tf_op jit(solution)/shard_map/ppermute | solution.py:18
  258.2 2.4 collective-permute-start.39
  260.6 4.1 %collective-permute-done.39 = f32[3,1,40,128]{3,2,1,0:T(8,128)S(1)} collective-permute-done((f32[3,1,40,128]{3,2,1,0:T(8,128)S(1)}, f32[3,1,40,128]{3,2,1,0:T(8,128)S(1)}, u32[]{:S(2)}, u32[]{:S(2)}) %collective-permute-start.39) | collective-permute-done | bytes 61472 | tf_op jit(solution)/shard_map/ppermute | solution.py:18
  266.7 3.9 %collective-permute-start.41 = (f32[3,18,1,128]{3,2,1,0:T(1,128)S(1)}, f32[3,18,1,128]{3,2,1,0:T(1,128)S(1)}, u32[]{:S(2)}, u32[]{:S(2)}) collective-permute-start(f32[3,18,1,128]{3,2,1,0:T(1,128)S(1)} %get-tuple-element.40), channel_id=1, source_target_pairs={{0,8},{8,16},{16,24},{24,32},{32,40},{40,48},{48,56},{56,64},{64,7... | collective-permute-start | bytes 82952 | tf_op jit(solution)/shard_map/ppermute | solution.py:18
  270.6 3.0 collective-permute-done.41
  277.6 1.9 collective-permute-start.42
  284.6 2.6 collective-permute-done.43
  288.9 4.2 %fusion.2 = f32[3,16,40,128]{3,2,1,0:T(8,128)S(1)} fusion(f32[3,16,40,128]{3,2,1,0:T(8,128)S(1)} %add_dynamic-update-slice_fusion, f32[3,18,42,1]{3,2,1,0:T(8,128)} %copy.269, f32[3,18,1,128]{3,2,1,0:T(1,128)S(1)} %collective-permute-done.40, f32[3,18,1,128]{3,2,1,0:T(1,128)S(1)} %collective-permute-done.41, ...), kind=kLoop, calls=%fused_computation.22 | loop fusion | flops 8601600 | bytes 4128480 | tf_op jit(solution)/shard_map/add | solution.py:56
  (243 shorter events, 71.1 us)
Async XLA Ops:
  7.2 127.2 %all-reduce.4.cloned.1.call-start = ((), (), s32[]{:S(2)}) async-start(), calls=%async_computation | async-start | bytes 245760 | tf_op jit(solution)/shard_map/psum | solution.py:133
  7.3 36.0 %collective-permute-start.6 = (f32[1,128]{1,0:T(1,128)S(1)}, f32[1,128]{1,0:T(1,128)S(1)}, u32[]{:S(2)}, u32[]{:S(2)}) collective-permute-start(f32[1,128]{1,0:T(1,128)S(1)} %broadcast.56), channel_id=1, source_target_pairs={{8,0},{16,8},{24,16},{32,24},{40,32},{48,40},{56,48},{64,56},{72,6... | collective-permute-start | bytes 1544 | tf_op jit(solution)/shard_map/ppermute | solution.py:20
  9.4 33.9 %collective-permute-start.7 = (f32[1,128]{1,0:T(1,128)S(1)}, f32[1,128]{1,0:T(1,128)S(1)}, u32[]{:S(2)}, u32[]{:S(2)}) collective-permute-start(f32[1,128]{1,0:T(1,128)S(1)} %broadcast.56), channel_id=1, source_target_pairs={{0,8},{8,16},{16,24},{24,32},{32,40},{40,48},{48,56},{56,64},{64,7... | collective-permute-start | bytes 1544 | tf_op jit(solution)/shard_map/ppermute | solution.py:18
  15.1 6.2 %collective-permute-start = (f32[4,1,40,128]{3,2,1,0:T(8,128)S(1)}, f32[4,1,40,128]{3,2,1,0:T(8,128)S(1)}, u32[]{:S(2)}, u32[]{:S(2)}) collective-permute-start(f32[4,1,40,128]{3,2,1,0:T(8,128)S(1)} %get-tuple-element.38), channel_id=1, source_target_pairs={{0,1},{1,2},{2,3},{3,4},{4,5},{5,6},{6,7},{8,9},{9,10},{10,11},{11... | collective-permute-start | bytes 245768 | tf_op jit(solution)/shard_map/ppermute | solution.py:18
  17.0 5.7 %collective-permute-start.1 = (f32[4,1,40,128]{3,2,1,0:T(8,128)S(1)}, f32[4,1,40,128]{3,2,1,0:T(8,128)S(1)}, u32[]{:S(2)}, u32[]{:S(2)}) collective-permute-start(f32[4,1,40,128]{3,2,1,0:T(8,128)S(1)} %get-tuple-element.39), channel_id=1, source_target_pairs={{1,0},{2,1},{3,2},{4,3},{5,4},{6,5},{7,6},{9,8},{10,9},{11,10},{12... | collective-permute-start | bytes 245768 | tf_op jit(solution)/shard_map/ppermute | solution.py:20
  22.8 7.8 %collective-permute-start.2 = (f32[4,18,1,128]{3,0,2,1:T(4,128)S(1)}, f32[4,18,1,128]{3,0,2,1:T(4,128)S(1)}, u32[]{:S(2)}, u32[]{:S(2)}) collective-permute-start(f32[4,18,1,128]{3,0,2,1:T(4,128)S(1)} %copy.276), channel_id=1, source_target_pairs={{0,8},{8,16},{16,24},{24,32},{32,40},{40,48},{48,56},{56,64},{64,7... | collective-permute-start | bytes 110600 | tf_op jit(solution)/shard_map/ppermute | solution.py:18
  26.6 5.9 %collective-permute-start.3 = (f32[4,18,1,128]{3,0,2,1:T(4,128)S(1)}, f32[4,18,1,128]{3,0,2,1:T(4,128)S(1)}, u32[]{:S(2)}, u32[]{:S(2)}) collective-permute-start(f32[4,18,1,128]{3,0,2,1:T(4,128)S(1)} %copy.277), channel_id=1, source_target_pairs={{8,0},{16,8},{24,16},{32,24},{40,32},{48,40},{56,48},{64,56},{72,6... | collective-permute-start | bytes 110600 | tf_op jit(solution)/shard_map/ppermute | solution.py:20
  36.7 6.6 %collective-permute-start.4 = (f32[4,18,42,1]{2,0,3,1:T(4,128)S(1)}, f32[4,18,42,1]{2,0,3,1:T(4,128)S(1)}, u32[]{:S(2)}, u32[]{:S(2)}) collective-permute-start(f32[4,18,42,1]{2,0,3,1:T(4,128)S(1)} %copy.246), channel_id=1, source_target_pairs={{0,128},{128,256},{256,384},{1,129},{129,257},{257,385},{2,130},{1... | collective-permute-start | bytes 36296 | tf_op jit(solution)/shard_map/ppermute | solution.py:18
  38.7 6.2 %collective-permute-start.5 = (f32[4,18,42,1]{2,0,3,1:T(4,128)S(1)}, f32[4,18,42,1]{2,0,3,1:T(4,128)S(1)}, u32[]{:S(2)}, u32[]{:S(2)}) collective-permute-start(f32[4,18,42,1]{2,0,3,1:T(4,128)S(1)} %copy.247), channel_id=1, source_target_pairs={{128,0},{256,128},{384,256},{129,1},{257,129},{385,257},{130,2},{2... | collective-permute-start | bytes 36296 | tf_op jit(solution)/shard_map/ppermute | solution.py:20
  54.5 80.0 %copy-start.48 = (f32[1,128]{1,0:T(1,128)S(1)}, f32[1,128]{1,0:T(1,128)}, u32[]{:S(2)}) copy-start(f32[1,128]{1,0:T(1,128)} %copy-done.47) | copy-start | bytes 1540
  54.5 80.0 %copy-start.50 = (f32[1,128]{1,0:T(1,128)S(1)}, f32[1,128]{1,0:T(1,128)}, u32[]{:S(2)}) copy-start(f32[1,128]{1,0:T(1,128)} %copy-done.49) | copy-start | bytes 1540
  57.4 5.7 %collective-permute-start.8 = (f32[42,1]{1,0:T(8,128)S(1)}, f32[42,1]{1,0:T(8,128)S(1)}, u32[]{:S(2)}, u32[]{:S(2)}) collective-permute-start(f32[42,1]{1,0:T(8,128)S(1)} %get-tuple-element.70), channel_id=1, source_target_pairs={{128,0},{256,128},{384,256},{129,1},{257,129},{385,257},{130,2},{2... | collective-permute-start | bytes 512 | tf_op jit(solution)/shard_map/ppermute | solution.py:20
  61.6 5.7 %collective-permute-start.9 = (f32[42,1]{1,0:T(8,128)S(1)}, f32[42,1]{1,0:T(8,128)S(1)}, u32[]{:S(2)}, u32[]{:S(2)}) collective-permute-start(f32[42,1]{1,0:T(8,128)S(1)} %get-tuple-element.71), channel_id=1, source_target_pairs={{0,128},{128,256},{256,384},{1,129},{129,257},{257,385},{2,130},{1... | collective-permute-start | bytes 512 | tf_op jit(solution)/shard_map/ppermute | solution.py:18
  134.4 88.6 %copy-start.4 = (f32[6,40,128]{2,1,0:T(8,128)S(1)}, f32[6,40,128]{2,1,0:T(8,128)}, u32[]{:S(2)}) copy-start(f32[6,40,128]{2,1,0:T(8,128)} %all-reduce.4.cloned.1.call-done) | copy-start | bytes 368644
  135.4 5.9 %collective-permute-start.10 = (f32[1,128]{1,0:T(1,128)S(1)}, f32[1,128]{1,0:T(1,128)S(1)}, u32[]{:S(2)}, u32[]{:S(2)}) collective-permute-start(f32[1,128]{1,0:T(1,128)S(1)} %get-tuple-element.85), channel_id=1, source_target_pairs={{8,0},{16,8},{24,16},{32,24},{40,32},{48,40},{56,48},{64,56},{72,6... | collective-permute-start | bytes 1544 | tf_op jit(solution)/shard_map/ppermute | solution.py:20
  137.8 6.6 %collective-permute-start.11 = (f32[1,128]{1,0:T(1,128)S(1)}, f32[1,128]{1,0:T(1,128)S(1)}, u32[]{:S(2)}, u32[]{:S(2)}) collective-permute-start(f32[1,128]{1,0:T(1,128)S(1)} %get-tuple-element.84), channel_id=1, source_target_pairs={{0,8},{8,16},{16,24},{24,32},{32,40},{40,48},{48,56},{56,64},{64,7... | collective-permute-start | bytes 1544 | tf_op jit(solution)/shard_map/ppermute | solution.py:18
  144.5 4.2 %collective-permute-start.12 = (f32[42,1]{1,0:T(8,128)S(1)}, f32[42,1]{1,0:T(8,128)S(1)}, u32[]{:S(2)}, u32[]{:S(2)}) collective-permute-start(f32[42,1]{1,0:T(8,128)S(1)} %get-tuple-element.68), channel_id=1, source_target_pairs={{128,0},{256,128},{384,256},{129,1},{257,129},{385,257},{130,2},{2... | collective-permute-start | bytes 512 | tf_op jit(solution)/shard_map/ppermute | solution.py:20
  147.2 5.7 %collective-permute-start.13 = (f32[42,1]{1,0:T(8,128)S(1)}, f32[42,1]{1,0:T(8,128)S(1)}, u32[]{:S(2)}, u32[]{:S(2)}) collective-permute-start(f32[42,1]{1,0:T(8,128)S(1)} %get-tuple-element.69), channel_id=1, source_target_pairs={{0,128},{128,256},{256,384},{1,129},{129,257},{257,385},{2,130},{1... | collective-permute-start | bytes 512 | tf_op jit(solution)/shard_map/ppermute | solution.py:18
  153.9 5.9 %collective-permute-start.14 = (f32[1,128]{1,0:T(1,128)S(1)}, f32[1,128]{1,0:T(1,128)S(1)}, u32[]{:S(2)}, u32[]{:S(2)}) collective-permute-start(f32[1,128]{1,0:T(1,128)S(1)} %get-tuple-element.83), channel_id=1, source_target_pairs={{8,0},{16,8},{24,16},{32,24},{40,32},{48,40},{56,48},{64,56},{72,6... | collective-permute-start | bytes 1544 | tf_op jit(solution)/shard_map/ppermute | solution.py:20
  155.8 6.6 %collective-permute-start.15 = (f32[1,128]{1,0:T(1,128)S(1)}, f32[1,128]{1,0:T(1,128)S(1)}, u32[]{:S(2)}, u32[]{:S(2)}) collective-permute-start(f32[1,128]{1,0:T(1,128)S(1)} %get-tuple-element.82), channel_id=1, source_target_pairs={{0,8},{8,16},{16,24},{24,32},{32,40},{40,48},{48,56},{56,64},{64,7... | collective-permute-start | bytes 1544 | tf_op jit(solution)/shard_map/ppermute | solution.py:18
  162.5 4.0 %collective-permute-start.16 = (f32[42,1]{1,0:T(8,128)S(1)}, f32[42,1]{1,0:T(8,128)S(1)}, u32[]{:S(2)}, u32[]{:S(2)}) collective-permute-start(f32[42,1]{1,0:T(8,128)S(1)} %get-tuple-element.66), channel_id=1, source_target_pairs={{128,0},{256,128},{384,256},{129,1},{257,129},{385,257},{130,2},{2... | collective-permute-start | bytes 512 | tf_op jit(solution)/shard_map/ppermute | solution.py:20
  165.0 5.7 %collective-permute-start.17 = (f32[42,1]{1,0:T(8,128)S(1)}, f32[42,1]{1,0:T(8,128)S(1)}, u32[]{:S(2)}, u32[]{:S(2)}) collective-permute-start(f32[42,1]{1,0:T(8,128)S(1)} %get-tuple-element.67), channel_id=1, source_target_pairs={{0,128},{128,256},{256,384},{1,129},{129,257},{257,385},{2,130},{1... | collective-permute-start | bytes 512 | tf_op jit(solution)/shard_map/ppermute | solution.py:18
  171.6 5.9 %collective-permute-start.18 = (f32[1,128]{1,0:T(1,128)S(1)}, f32[1,128]{1,0:T(1,128)S(1)}, u32[]{:S(2)}, u32[]{:S(2)}) collective-permute-start(f32[1,128]{1,0:T(1,128)S(1)} %get-tuple-element.81), channel_id=1, source_target_pairs={{8,0},{16,8},{24,16},{32,24},{40,32},{48,40},{56,48},{64,56},{72,6... | collective-permute-start | bytes 1544 | tf_op jit(solution)/shard_map/ppermute | solution.py:20
  173.6 6.6 %collective-permute-start.19 = (f32[1,128]{1,0:T(1,128)S(1)}, f32[1,128]{1,0:T(1,128)S(1)}, u32[]{:S(2)}, u32[]{:S(2)}) collective-permute-start(f32[1,128]{1,0:T(1,128)S(1)} %get-tuple-element.80), channel_id=1, source_target_pairs={{0,8},{8,16},{16,24},{24,32},{32,40},{40,48},{48,56},{56,64},{64,7... | collective-permute-start | bytes 1544 | tf_op jit(solution)/shard_map/ppermute | solution.py:18
  180.3 3.9 %collective-permute-start.20 = (f32[42,1]{1,0:T(8,128)S(1)}, f32[42,1]{1,0:T(8,128)S(1)}, u32[]{:S(2)}, u32[]{:S(2)}) collective-permute-start(f32[42,1]{1,0:T(8,128)S(1)} %get-tuple-element.64), channel_id=1, source_target_pairs={{128,0},{256,128},{384,256},{129,1},{257,129},{385,257},{130,2},{2... | collective-permute-start | bytes 512 | tf_op jit(solution)/shard_map/ppermute | solution.py:20
  182.7 5.7 %collective-permute-start.21 = (f32[42,1]{1,0:T(8,128)S(1)}, f32[42,1]{1,0:T(8,128)S(1)}, u32[]{:S(2)}, u32[]{:S(2)}) collective-permute-start(f32[42,1]{1,0:T(8,128)S(1)} %get-tuple-element.65), channel_id=1, source_target_pairs={{0,128},{128,256},{256,384},{1,129},{129,257},{257,385},{2,130},{1... | collective-permute-start | bytes 512 | tf_op jit(solution)/shard_map/ppermute | solution.py:18
  189.4 6.0 %collective-permute-start.22 = (f32[1,128]{1,0:T(1,128)S(1)}, f32[1,128]{1,0:T(1,128)S(1)}, u32[]{:S(2)}, u32[]{:S(2)}) collective-permute-start(f32[1,128]{1,0:T(1,128)S(1)} %get-tuple-element.79), channel_id=1, source_target_pairs={{8,0},{16,8},{24,16},{32,24},{40,32},{48,40},{56,48},{64,56},{72,6... | collective-permute-start | bytes 1544 | tf_op jit(solution)/shard_map/ppermute | solution.py:20
  191.5 6.6 %collective-permute-start.23 = (f32[1,128]{1,0:T(1,128)S(1)}, f32[1,128]{1,0:T(1,128)S(1)}, u32[]{:S(2)}, u32[]{:S(2)}) collective-permute-start(f32[1,128]{1,0:T(1,128)S(1)} %get-tuple-element.78), channel_id=1, source_target_pairs={{0,8},{8,16},{16,24},{24,32},{32,40},{40,48},{48,56},{56,64},{64,7... | collective-permute-start | bytes 1544 | tf_op jit(solution)/shard_map/ppermute | solution.py:18
  198.2 3.4 %collective-permute-start.24 = (f32[42,1]{1,0:T(8,128)S(1)}, f32[42,1]{1,0:T(8,128)S(1)}, u32[]{:S(2)}, u32[]{:S(2)}) collective-permute-start(f32[42,1]{1,0:T(8,128)S(1)} %get-tuple-element.62), channel_id=1, source_target_pairs={{128,0},{256,128},{384,256},{129,1},{257,129},{385,257},{130,2},{2... | collective-permute-start | bytes 512 | tf_op jit(solution)/shard_map/ppermute | solution.py:20
  200.1 5.7 %collective-permute-start.25 = (f32[42,1]{1,0:T(8,128)S(1)}, f32[42,1]{1,0:T(8,128)S(1)}, u32[]{:S(2)}, u32[]{:S(2)}) collective-permute-start(f32[42,1]{1,0:T(8,128)S(1)} %get-tuple-element.63), channel_id=1, source_target_pairs={{0,128},{128,256},{256,384},{1,129},{129,257},{257,385},{2,130},{1... | collective-permute-start | bytes 512 | tf_op jit(solution)/shard_map/ppermute | solution.py:18
  206.8 5.9 %collective-permute-start.26 = (f32[1,128]{1,0:T(1,128)S(1)}, f32[1,128]{1,0:T(1,128)S(1)}, u32[]{:S(2)}, u32[]{:S(2)}) collective-permute-start(f32[1,128]{1,0:T(1,128)S(1)} %get-tuple-element.77), channel_id=1, source_target_pairs={{8,0},{16,8},{24,16},{32,24},{40,32},{48,40},{56,48},{64,56},{72,6... | collective-permute-start | bytes 1544 | tf_op jit(solution)/shard_map/ppermute | solution.py:20
  208.7 6.6 %collective-permute-start.27 = (f32[1,128]{1,0:T(1,128)S(1)}, f32[1,128]{1,0:T(1,128)S(1)}, u32[]{:S(2)}, u32[]{:S(2)}) collective-permute-start(f32[1,128]{1,0:T(1,128)S(1)} %get-tuple-element.76), channel_id=1, source_target_pairs={{0,8},{8,16},{16,24},{24,32},{32,40},{40,48},{48,56},{56,64},{64,7... | collective-permute-start | bytes 1544 | tf_op jit(solution)/shard_map/ppermute | solution.py:18
  215.4 3.4 %collective-permute-start.28 = (f32[42,1]{1,0:T(8,128)S(1)}, f32[42,1]{1,0:T(8,128)S(1)}, u32[]{:S(2)}, u32[]{:S(2)}) collective-permute-start(f32[42,1]{1,0:T(8,128)S(1)} %get-tuple-element.60), channel_id=1, source_target_pairs={{128,0},{256,128},{384,256},{129,1},{257,129},{385,257},{130,2},{2... | collective-permute-start | bytes 512 | tf_op jit(solution)/shard_map/ppermute | solution.py:20
  217.3 5.7 %collective-permute-start.29 = (f32[42,1]{1,0:T(8,128)S(1)}, f32[42,1]{1,0:T(8,128)S(1)}, u32[]{:S(2)}, u32[]{:S(2)}) collective-permute-start(f32[42,1]{1,0:T(8,128)S(1)} %get-tuple-element.61), channel_id=1, source_target_pairs={{0,128},{128,256},{256,384},{1,129},{129,257},{257,385},{2,130},{1... | collective-permute-start | bytes 512 | tf_op jit(solution)/shard_map/ppermute | solution.py:18
  223.2 5.9 %collective-permute-start.30 = (f32[1,128]{1,0:T(1,128)S(1)}, f32[1,128]{1,0:T(1,128)S(1)}, u32[]{:S(2)}, u32[]{:S(2)}) collective-permute-start(f32[1,128]{1,0:T(1,128)S(1)} %get-tuple-element.75), channel_id=1, source_target_pairs={{8,0},{16,8},{24,16},{32,24},{40,32},{48,40},{56,48},{64,56},{72,6... | collective-permute-start | bytes 1544 | tf_op jit(solution)/shard_map/ppermute | solution.py:20
  225.1 6.6 %collective-permute-start.31 = (f32[1,128]{1,0:T(1,128)S(1)}, f32[1,128]{1,0:T(1,128)S(1)}, u32[]{:S(2)}, u32[]{:S(2)}) collective-permute-start(f32[1,128]{1,0:T(1,128)S(1)} %get-tuple-element.74), channel_id=1, source_target_pairs={{0,8},{8,16},{16,24},{24,32},{32,40},{40,48},{48,56},{56,64},{64,7... | collective-permute-start | bytes 1544 | tf_op jit(solution)/shard_map/ppermute | solution.py:18
  231.8 3.4 %collective-permute-start.32 = (f32[42,1]{1,0:T(8,128)S(1)}, f32[42,1]{1,0:T(8,128)S(1)}, u32[]{:S(2)}, u32[]{:S(2)}) collective-permute-start(f32[42,1]{1,0:T(8,128)S(1)} %get-tuple-element.58), channel_id=1, source_target_pairs={{128,0},{256,128},{384,256},{129,1},{257,129},{385,257},{130,2},{2... | collective-permute-start | bytes 512 | tf_op jit(solution)/shard_map/ppermute | solution.py:20
  233.8 5.7 %collective-permute-start.33 = (f32[42,1]{1,0:T(8,128)S(1)}, f32[42,1]{1,0:T(8,128)S(1)}, u32[]{:S(2)}, u32[]{:S(2)}) collective-permute-start(f32[42,1]{1,0:T(8,128)S(1)} %get-tuple-element.59), channel_id=1, source_target_pairs={{0,128},{128,256},{256,384},{1,129},{129,257},{257,385},{2,130},{1... | collective-permute-start | bytes 512 | tf_op jit(solution)/shard_map/ppermute | solution.py:18
  239.6 5.9 %collective-permute-start.34 = (f32[1,128]{1,0:T(1,128)S(1)}, f32[1,128]{1,0:T(1,128)S(1)}, u32[]{:S(2)}, u32[]{:S(2)}) collective-permute-start(f32[1,128]{1,0:T(1,128)S(1)} %get-tuple-element.73), channel_id=1, source_target_pairs={{8,0},{16,8},{24,16},{32,24},{40,32},{48,40},{56,48},{64,56},{72,6... | collective-permute-start | bytes 1544 | tf_op jit(solution)/shard_map/ppermute | solution.py:20
  241.5 6.6 %collective-permute-start.35 = (f32[1,128]{1,0:T(1,128)S(1)}, f32[1,128]{1,0:T(1,128)S(1)}, u32[]{:S(2)}, u32[]{:S(2)}) collective-permute-start(f32[1,128]{1,0:T(1,128)S(1)} %get-tuple-element.72), channel_id=1, source_target_pairs={{0,8},{8,16},{16,24},{24,32},{32,40},{40,48},{48,56},{56,64},{64,7... | collective-permute-start | bytes 1544 | tf_op jit(solution)/shard_map/ppermute | solution.py:18
  248.2 3.6 %collective-permute-start.36 = (f32[42,1]{1,0:T(8,128)S(1)}, f32[42,1]{1,0:T(8,128)S(1)}, u32[]{:S(2)}, u32[]{:S(2)}) collective-permute-start(f32[42,1]{1,0:T(8,128)S(1)} %get-tuple-element.56), channel_id=1, source_target_pairs={{128,0},{256,128},{384,256},{129,1},{257,129},{385,257},{130,2},{2... | collective-permute-start | bytes 512 | tf_op jit(solution)/shard_map/ppermute | solution.py:20
  250.3 5.7 %collective-permute-start.37 = (f32[42,1]{1,0:T(8,128)S(1)}, f32[42,1]{1,0:T(8,128)S(1)}, u32[]{:S(2)}, u32[]{:S(2)}) collective-permute-start(f32[42,1]{1,0:T(8,128)S(1)} %get-tuple-element.57), channel_id=1, source_target_pairs={{0,128},{128,256},{256,384},{1,129},{129,257},{257,385},{2,130},{1... | collective-permute-start | bytes 512 | tf_op jit(solution)/shard_map/ppermute | solution.py:18
  256.2 4.3 %collective-permute-start.38 = (f32[3,1,40,128]{3,2,1,0:T(8,128)S(1)}, f32[3,1,40,128]{3,2,1,0:T(8,128)S(1)}, u32[]{:S(2)}, u32[]{:S(2)}) collective-permute-start(f32[3,1,40,128]{3,2,1,0:T(8,128)S(1)} %get-tuple-element.43), channel_id=1, source_target_pairs={{1,0},{2,1},{3,2},{4,3},{5,4},{6,5},{7,6},{9,8},{10,9},{11,10},{12... | collective-permute-start | bytes 184328 | tf_op jit(solution)/shard_map/ppermute | solution.py:20
  258.2 6.6 %collective-permute-start.39 = (f32[3,1,40,128]{3,2,1,0:T(8,128)S(1)}, f32[3,1,40,128]{3,2,1,0:T(8,128)S(1)}, u32[]{:S(2)}, u32[]{:S(2)}) collective-permute-start(f32[3,1,40,128]{3,2,1,0:T(8,128)S(1)} %get-tuple-element.42), channel_id=1, source_target_pairs={{0,1},{1,2},{2,3},{3,4},{4,5},{5,6},{6,7},{8,9},{9,10},{10,11},{11... | collective-permute-start | bytes 184328 | tf_op jit(solution)/shard_map/ppermute | solution.py:18
  264.8 5.9 %collective-permute-start.40 = (f32[3,18,1,128]{3,2,1,0:T(1,128)S(1)}, f32[3,18,1,128]{3,2,1,0:T(1,128)S(1)}, u32[]{:S(2)}, u32[]{:S(2)}) collective-permute-start(f32[3,18,1,128]{3,2,1,0:T(1,128)S(1)} %get-tuple-element.41), channel_id=1, source_target_pairs={{8,0},{16,8},{24,16},{32,24},{40,32},{48,40},{56,48},{64,56},{72,6... | collective-permute-start | bytes 82952 | tf_op jit(solution)/shard_map/ppermute | solution.py:20
  266.7 7.0 %collective-permute-start.41 = (f32[3,18,1,128]{3,2,1,0:T(1,128)S(1)}, f32[3,18,1,128]{3,2,1,0:T(1,128)S(1)}, u32[]{:S(2)}, u32[]{:S(2)}) collective-permute-start(f32[3,18,1,128]{3,2,1,0:T(1,128)S(1)} %get-tuple-element.40), channel_id=1, source_target_pairs={{0,8},{8,16},{16,24},{24,32},{32,40},{40,48},{48,56},{56,64},{64,7... | collective-permute-start | bytes 82952 | tf_op jit(solution)/shard_map/ppermute | solution.py:18
  277.6 5.4 %collective-permute-start.42 = (f32[3,18,42,1]{2,3,1,0:T(1,128)S(1)}, f32[3,18,42,1]{2,3,1,0:T(1,128)S(1)}, u32[]{:S(2)}, u32[]{:S(2)}) collective-permute-start(f32[3,18,42,1]{2,3,1,0:T(1,128)S(1)} %copy.278), channel_id=1, source_target_pairs={{128,0},{256,128},{384,256},{129,1},{257,129},{385,257},{130,2},{2... | collective-permute-start | bytes 27224 | tf_op jit(solution)/shard_map/ppermute | solution.py:20
  281.5 5.8 %collective-permute-start.43 = (f32[3,18,42,1]{2,3,1,0:T(1,128)S(1)}, f32[3,18,42,1]{2,3,1,0:T(1,128)S(1)}, u32[]{:S(2)}, u32[]{:S(2)}) collective-permute-start(f32[3,18,42,1]{2,3,1,0:T(1,128)S(1)} %copy.279), channel_id=1, source_target_pairs={{0,128},{128,256},{256,384},{1,129},{129,257},{257,385},{2,130},{1... | collective-permute-start | bytes 27224 | tf_op jit(solution)/shard_map/ppermute | solution.py:18
  (49 other events, 272.5 us)
Sparse Core Ops, SparseCore 0:
  57.4 76.9 all-reduce.3
where the time goes:
time: 309 us; the launch traced here: 307 us
  waiting for transfers between devices  136 us (44%)
  starting transfers between devices  109 us (35%)
  other arithmetic  23.4 us (8%)
  local copies, waits for them, and re-layouts  22.7 us (7%)
  between operations  15.3 us (5%)
    psum x1, waiting for transfers between devices, per_device(): totals = lax.psum(planes, 'gz')  67.1 us
    ppermute x22, waiting for transfers between devices, extended(): lax.ppermute(tail, axis, [(i, (i + 1) % count) for i in range(ends)])  62.9 us
    ppermute x22, starting transfers between devices, extended(): lax.ppermute(tail, axis, [(i, (i + 1) % count) for i in range(ends)])  56 us
    ppermute x22, starting transfers between devices, extended(): lax.ppermute(head, axis, [((i + 1) % count, i) for i in range(ends)])  53 us
    unnamed x121, local copies, waits for them, and re-layouts  8.34 us
    add x2, other arithmetic, apply_operator(): fluxes = fluxes + weight[None] * (center - nearby)  7.53 us
  transfers between devices with their start and end apart: 45, of which 30 were waited for; matrix products, arithmetic and copies ran while one was open for 4% of the time, Pallas kernels for 0%

commit v1 on v0

--- a/solution.py
+++ b/solution.py
@@ -130,7 +130,9 @@
         padded[:3], weights, storage, storage_rows, coupling_rows
     )
     planes = coarse_planes(residual, weights, storage, storage_rows, coupling_rows)
-    totals = lax.psum(planes, "gz")
+    totals = planes
+    for hop in (1, 2, 4):
+        totals = totals + lax.ppermute(totals, "gz", [(dev, dev ^ hop) for dev in range(8)])
     correction = jnp.zeros(totals.shape[1:], jnp.float32)
     for repeat_index in range(SWEEPS):
         bordered = extended(correction, (("gy", 0), ("gx", 1)), 1)

time: 309 us -> 238 us (0.77)
  the two profiles are of different devices: /device:TPU:154 before, /device:TPU:410 now
where the time goes in v1:
time: 238 us; the launch traced here: 236 us
  starting transfers between devices  120 us (50%)
  waiting for transfers between devices  72.5 us (30%)
  local copies, waits for them, and re-layouts  22.1 us (9%)
  other arithmetic  19.4 us (8%)
    ppermute x22, waiting for transfers between devices, extended(): lax.ppermute(tail, axis, [(i, (i + 1) % count) for i in range(ends)])  65 us
    ppermute x22, starting transfers between devices, extended(): lax.ppermute(head, axis, [((i + 1) % count, i) for i in range(ends)])  59.8 us
    ppermute x22, starting transfers between devices, extended(): lax.ppermute(tail, axis, [(i, (i + 1) % count) for i in range(ends)])  51.1 us
    ppermute x3, starting transfers between devices, per_device(): lax.ppermute(totals, 'gz', [(dev, dev ^ hop) for dev in range(8)])  8.96 us
    unnamed x101, local copies, waits for them, and re-layouts  7.68 us
    add x2, other arithmetic, apply_operator(): fluxes = fluxes + weight[None] * (center - nearby)  7.53 us
    ppermute x22, waiting for transfers between devices, extended(): lax.ppermute(head, axis, [((i + 1) % count, i) for i in range(ends)])  6.17 us
    slice x11, local copies, waits for them, and re-layouts, extended(): head = lax.slice_in_dim(cells, 0, width, axis=dim)  4.98 us
  transfers between devices with their start and end apart: 47, of which 31 were waited for; matrix products, arithmetic and copies ran while one was open for 3% of the time, Pallas kernels for 0%

profile of v1, /device:TPU:410, one launch (start us, length us, event | category | flops | bytes accessed | tf_op | source)
XLA Modules:
  0.0 236.1 jit_solution(12717379455563897689)
XLA Ops:
  2.6 1.9 collective-permute-start
  4.5 3.6 %collective-permute-start.1 = (f32[4,1,40,128]{3,2,1,0:T(8,128)S(1)}, f32[4,1,40,128]{3,2,1,0:T(8,128)S(1)}, u32[]{:S(2)}, u32[]{:S(2)}) collective-permute-start(f32[4,1,40,128]{3,2,1,0:T(8,128)S(1)} %get-tuple-element.39), channel_id=1, source_target_pairs={{1,0},{2,1},{3,2},{4,3},{5,4},{6,5},{7,6},{9,8},{10,9},{11,10},{12... | collective-permute-start | bytes 245768 | tf_op jit(solution)/shard_map/ppermute | solution.py:20
  10.3 2.9 %collective-permute-start.2 = (f32[4,18,1,128]{3,0,2,1:T(4,128)S(1)}, f32[4,18,1,128]{3,0,2,1:T(4,128)S(1)}, u32[]{:S(2)}, u32[]{:S(2)}) collective-permute-start(f32[4,18,1,128]{3,0,2,1:T(4,128)S(1)} %copy.276), channel_id=1, source_target_pairs={{0,8},{8,16},{16,24},{24,32},{32,40},{40,48},{48,56},{56,64},{64,7... | collective-permute-start | bytes 110600 | tf_op jit(solution)/shard_map/ppermute | solution.py:18
  13.2 4.1 %collective-permute-start.3 = (f32[4,18,1,128]{3,0,2,1:T(4,128)S(1)}, f32[4,18,1,128]{3,0,2,1:T(4,128)S(1)}, u32[]{:S(2)}, u32[]{:S(2)}) collective-permute-start(f32[4,18,1,128]{3,0,2,1:T(4,128)S(1)} %copy.277), channel_id=1, source_target_pairs={{8,0},{16,8},{24,16},{32,24},{40,32},{48,40},{56,48},{64,56},{72,6... | collective-permute-start | bytes 110600 | tf_op jit(solution)/shard_map/ppermute | solution.py:20
  21.2 2.2 copy.246
  25.3 4.5 %collective-permute-start.5 = (f32[4,18,42,1]{2,0,3,1:T(4,128)S(1)}, f32[4,18,42,1]{2,0,3,1:T(4,128)S(1)}, u32[]{:S(2)}, u32[]{:S(2)}) collective-permute-start(f32[4,18,42,1]{2,0,3,1:T(4,128)S(1)} %copy.247), channel_id=1, source_target_pairs={{128,0},{256,128},{384,256},{129,1},{257,129},{385,257},{130,2},{2... | collective-permute-start | bytes 36296 | tf_op jit(solution)/shard_map/ppermute | solution.py:20
  36.4 3.3 %fusion.19 = f32[3,16,40,128]{3,2,1,0:T(8,128)S(1)} fusion(f32[3,16,40,128]{3,2,1,0:T(8,128)S(1)} %copy-done, f32[4,18,42,1]{3,2,1,0:T(8,128)S(1)} %copy.248, f32[4,18,1,128]{3,2,1,0:T(1,128)S(1)} %copy.245, f32[4,18,1,128]{3,2,1,0:T(1,128)S(1)} %copy.244, f32[4,1,40,128]{3,2,1,0:T(8,128)S(1)} %collective-permute-done.1, ...), kind=kLoop, calls=%fused_computation.57 | loop fusion | flops 10076160 | bytes 4521600 | tf_op jit(solution)/shard_map/add | solution.py:56
  43.2 1.9 collective-permute-start.6
  46.5 1.9 collective-permute-start.7
  48.4 2.9 %collective-permute-start.10 = (f32[1,128]{1,0:T(1,128)S(1)}, f32[1,128]{1,0:T(1,128)S(1)}, u32[]{:S(2)}, u32[]{:S(2)}) collective-permute-start(f32[1,128]{1,0:T(1,128)S(1)} %broadcast.56), channel_id=1, source_target_pairs={{0,8},{8,16},{16,24},{24,32},{32,40},{40,48},{48,56},{56,64},{64,7... | collective-permute-start | bytes 1544 | tf_op jit(solution)/shard_map/ppermute | solution.py:18
  51.3 4.3 %collective-permute-start.9 = (f32[1,128]{1,0:T(1,128)S(1)}, f32[1,128]{1,0:T(1,128)S(1)}, u32[]{:S(2)}, u32[]{:S(2)}) collective-permute-start(f32[1,128]{1,0:T(1,128)S(1)} %broadcast.56), channel_id=1, source_target_pairs={{8,0},{16,8},{24,16},{32,24},{40,32},{48,40},{56,48},{64,56},{72,6... | collective-permute-start | bytes 1544 | tf_op jit(solution)/shard_map/ppermute | solution.py:20
  57.0 5.1 %collective-permute-start.8 = (f32[6,40,128]{2,1,0:T(8,128)S(1)}, f32[6,40,128]{2,1,0:T(8,128)S(1)}, u32[]{:S(2)}, u32[]{:S(2)}) collective-permute-start(f32[6,40,128]{2,1,0:T(8,128)S(1)} %add.411), channel_id=1, source_target_pairs={{0,4},{1,5},{2,6},{3,7},{4,0},{5,1},{6,2},{7,3},{8,12},{9,13},{10,... | collective-permute-start | bytes 368648 | tf_op jit(solution)/shard_map/ppermute | solution.py:135
  62.2 4.2 %collective-permute-start.11 = (f32[42,1]{1,0:T(8,128)S(1)}, f32[42,1]{1,0:T(8,128)S(1)}, u32[]{:S(2)}, u32[]{:S(2)}) collective-permute-start(f32[42,1]{1,0:T(8,128)S(1)} %get-tuple-element.70), channel_id=1, source_target_pairs={{128,0},{256,128},{384,256},{129,1},{257,129},{385,257},{130,2},{2... | collective-permute-start | bytes 512 | tf_op jit(solution)/shard_map/ppermute | solution.py:20
  67.9 4.2 %collective-permute-done.12 = f32[42,1]{1,0:T(8,128)S(1)} collective-permute-done((f32[42,1]{1,0:T(8,128)S(1)}, f32[42,1]{1,0:T(8,128)S(1)}, u32[]{:S(2)}, u32[]{:S(2)}) %collective-permute-start.12) | collective-permute-done | bytes 200 | tf_op jit(solution)/shard_map/ppermute | solution.py:18
  72.2 5.4 %collective-permute-start.13 = (f32[1,128]{1,0:T(1,128)S(1)}, f32[1,128]{1,0:T(1,128)S(1)}, u32[]{:S(2)}, u32[]{:S(2)}) collective-permute-start(f32[1,128]{1,0:T(1,128)S(1)} %get-tuple-element.85), channel_id=1, source_target_pairs={{8,0},{16,8},{24,16},{32,24},{40,32},{48,40},{56,48},{64,56},{72,6... | collective-permute-start | bytes 1544 | tf_op jit(solution)/shard_map/ppermute | solution.py:20
  77.6 1.9 collective-permute-start.14
  79.6 4.7 %collective-permute-done.14 = f32[1,128]{1,0:T(1,128)S(1)} collective-permute-done((f32[1,128]{1,0:T(1,128)S(1)}, f32[1,128]{1,0:T(1,128)S(1)}, u32[]{:S(2)}, u32[]{:S(2)}) %collective-permute-start.14) | collective-permute-done | bytes 544 | tf_op jit(solution)/shard_map/ppermute | solution.py:18
  84.3 2.6 %collective-permute-start.15 = (f32[42,1]{1,0:T(8,128)S(1)}, f32[42,1]{1,0:T(8,128)S(1)}, u32[]{:S(2)}, u32[]{:S(2)}) collective-permute-start(f32[42,1]{1,0:T(8,128)S(1)} %get-tuple-element.68), channel_id=1, source_target_pairs={{128,0},{256,128},{384,256},{129,1},{257,129},{385,257},{130,2},{2... | collective-permute-start | bytes 512 | tf_op jit(solution)/shard_map/ppermute | solution.py:20
  88.5 4.2 %collective-permute-done.16 = f32[42,1]{1,0:T(8,128)S(1)} collective-permute-done((f32[42,1]{1,0:T(8,128)S(1)}, f32[42,1]{1,0:T(8,128)S(1)}, u32[]{:S(2)}, u32[]{:S(2)}) %collective-permute-start.16) | collective-permute-done | bytes 200 | tf_op jit(solution)/shard_map/ppermute | solution.py:18
  92.8 1.9 collective-permute-start.17
  94.8 3.9 %collective-permute-start.18 = (f32[1,128]{1,0:T(1,128)S(1)}, f32[1,128]{1,0:T(1,128)S(1)}, u32[]{:S(2)}, u32[]{:S(2)}) collective-permute-start(f32[1,128]{1,0:T(1,128)S(1)} %get-tuple-element.82), channel_id=1, source_target_pairs={{0,8},{8,16},{16,24},{24,32},{32,40},{40,48},{48,56},{56,64},{64,7... | collective-permute-start | bytes 1544 | tf_op jit(solution)/shard_map/ppermute | solution.py:18
  98.7 2.7 %collective-permute-done.18 = f32[1,128]{1,0:T(1,128)S(1)} collective-permute-done((f32[1,128]{1,0:T(1,128)S(1)}, f32[1,128]{1,0:T(1,128)S(1)}, u32[]{:S(2)}, u32[]{:S(2)}) %collective-permute-start.18) | collective-permute-done | bytes 544 | tf_op jit(solution)/shard_map/ppermute | solution.py:18
  101.5 2.3 collective-permute-start.19
  105.3 4.2 %collective-permute-done.20 = f32[42,1]{1,0:T(8,128)S(1)} collective-permute-done((f32[42,1]{1,0:T(8,128)S(1)}, f32[42,1]{1,0:T(8,128)S(1)}, u32[]{:S(2)}, u32[]{:S(2)}) %collective-permute-start.20) | collective-permute-done | bytes 200 | tf_op jit(solution)/shard_map/ppermute | solution.py:18
  111.6 3.9 %collective-permute-start.22 = (f32[1,128]{1,0:T(1,128)S(1)}, f32[1,128]{1,0:T(1,128)S(1)}, u32[]{:S(2)}, u32[]{:S(2)}) collective-permute-start(f32[1,128]{1,0:T(1,128)S(1)} %get-tuple-element.80), channel_id=1, source_target_pairs={{0,8},{8,16},{16,24},{24,32},{32,40},{40,48},{48,56},{56,64},{64,7... | collective-permute-start | bytes 1544 | tf_op jit(solution)/shard_map/ppermute | solution.py:18
  115.5 2.7 %collective-permute-done.22 = f32[1,128]{1,0:T(1,128)S(1)} collective-permute-done((f32[1,128]{1,0:T(1,128)S(1)}, f32[1,128]{1,0:T(1,128)S(1)}, u32[]{:S(2)}, u32[]{:S(2)}) %collective-permute-start.22) | collective-permute-done | bytes 544 | tf_op jit(solution)/shard_map/ppermute | solution.py:18
  121.8 4.2 %collective-permute-done.24 = f32[42,1]{1,0:T(8,128)S(1)} collective-permute-done((f32[42,1]{1,0:T(8,128)S(1)}, f32[42,1]{1,0:T(8,128)S(1)}, u32[]{:S(2)}, u32[]{:S(2)}) %collective-permute-start.24) | collective-permute-done | bytes 200 | tf_op jit(solution)/shard_map/ppermute | solution.py:18
  126.1 2.8 %collective-permute-start.25 = (f32[1,128]{1,0:T(1,128)S(1)}, f32[1,128]{1,0:T(1,128)S(1)}, u32[]{:S(2)}, u32[]{:S(2)}) collective-permute-start(f32[1,128]{1,0:T(1,128)S(1)} %get-tuple-element.79), channel_id=1, source_target_pairs={{8,0},{16,8},{24,16},{32,24},{40,32},{48,40},{56,48},{64,56},{72,6... | collective-permute-start | bytes 1544 | tf_op jit(solution)/shard_map/ppermute | solution.py:20
  128.9 3.2 %collective-permute-start.26 = (f32[1,128]{1,0:T(1,128)S(1)}, f32[1,128]{1,0:T(1,128)S(1)}, u32[]{:S(2)}, u32[]{:S(2)}) collective-permute-start(f32[1,128]{1,0:T(1,128)S(1)} %get-tuple-element.78), channel_id=1, source_target_pairs={{0,8},{8,16},{16,24},{24,32},{32,40},{40,48},{48,56},{56,64},{64,7... | collective-permute-start | bytes 1544 | tf_op jit(solution)/shard_map/ppermute | solution.py:18
  132.1 3.5 %collective-permute-done.26 = f32[1,128]{1,0:T(1,128)S(1)} collective-permute-done((f32[1,128]{1,0:T(1,128)S(1)}, f32[1,128]{1,0:T(1,128)S(1)}, u32[]{:S(2)}, u32[]{:S(2)}) %collective-permute-start.26) | collective-permute-done | bytes 544 | tf_op jit(solution)/shard_map/ppermute | solution.py:18
  139.1 4.2 %collective-permute-done.28 = f32[42,1]{1,0:T(8,128)S(1)} collective-permute-done((f32[42,1]{1,0:T(8,128)S(1)}, f32[42,1]{1,0:T(8,128)S(1)}, u32[]{:S(2)}, u32[]{:S(2)}) %collective-permute-start.28) | collective-permute-done | bytes 200 | tf_op jit(solution)/shard_map/ppermute | solution.py:18
  143.4 2.7 %collective-permute-start.29 = (f32[1,128]{1,0:T(1,128)S(1)}, f32[1,128]{1,0:T(1,128)S(1)}, u32[]{:S(2)}, u32[]{:S(2)}) collective-permute-start(f32[1,128]{1,0:T(1,128)S(1)} %get-tuple-element.77), channel_id=1, source_target_pairs={{8,0},{16,8},{24,16},{32,24},{40,32},{48,40},{56,48},{64,56},{72,6... | collective-permute-start | bytes 1544 | tf_op jit(solution)/shard_map/ppermute | solution.py:20
  146.1 3.1 %collective-permute-start.30 = (f32[1,128]{1,0:T(1,128)S(1)}, f32[1,128]{1,0:T(1,128)S(1)}, u32[]{:S(2)}, u32[]{:S(2)}) collective-permute-start(f32[1,128]{1,0:T(1,128)S(1)} %get-tuple-element.76), channel_id=1, source_target_pairs={{0,8},{8,16},{16,24},{24,32},{32,40},{40,48},{48,56},{56,64},{64,7... | collective-permute-start | bytes 1544 | tf_op jit(solution)/shard_map/ppermute | solution.py:18
  149.3 3.5 %collective-permute-done.30 = f32[1,128]{1,0:T(1,128)S(1)} collective-permute-done((f32[1,128]{1,0:T(1,128)S(1)}, f32[1,128]{1,0:T(1,128)S(1)}, u32[]{:S(2)}, u32[]{:S(2)}) %collective-permute-start.30) | collective-permute-done | bytes 544 | tf_op jit(solution)/shard_map/ppermute | solution.py:18
  156.3 4.2 %collective-permute-done.32 = f32[42,1]{1,0:T(8,128)S(1)} collective-permute-done((f32[42,1]{1,0:T(8,128)S(1)}, f32[42,1]{1,0:T(8,128)S(1)}, u32[]{:S(2)}, u32[]{:S(2)}) %collective-permute-start.32) | collective-permute-done | bytes 200 | tf_op jit(solution)/shard_map/ppermute | solution.py:18
  162.5 3.9 %collective-permute-start.34 = (f32[1,128]{1,0:T(1,128)S(1)}, f32[1,128]{1,0:T(1,128)S(1)}, u32[]{:S(2)}, u32[]{:S(2)}) collective-permute-start(f32[1,128]{1,0:T(1,128)S(1)} %get-tuple-element.74), channel_id=1, source_target_pairs={{0,8},{8,16},{16,24},{24,32},{32,40},{40,48},{48,56},{56,64},{64,7... | collective-permute-start | bytes 1544 | tf_op jit(solution)/shard_map/ppermute | solution.py:18
  166.5 2.7 %collective-permute-done.34 = f32[1,128]{1,0:T(1,128)S(1)} collective-permute-done((f32[1,128]{1,0:T(1,128)S(1)}, f32[1,128]{1,0:T(1,128)S(1)}, u32[]{:S(2)}, u32[]{:S(2)}) %collective-permute-start.34) | collective-permute-done | bytes 544 | tf_op jit(solution)/shard_map/ppermute | solution.py:18
  172.7 4.2 %collective-permute-done.36 = f32[42,1]{1,0:T(8,128)S(1)} collective-permute-done((f32[42,1]{1,0:T(8,128)S(1)}, f32[42,1]{1,0:T(8,128)S(1)}, u32[]{:S(2)}, u32[]{:S(2)}) %collective-permute-start.36) | collective-permute-done | bytes 200 | tf_op jit(solution)/shard_map/ppermute | solution.py:18
  178.9 3.9 %collective-permute-start.38 = (f32[1,128]{1,0:T(1,128)S(1)}, f32[1,128]{1,0:T(1,128)S(1)}, u32[]{:S(2)}, u32[]{:S(2)}) collective-permute-start(f32[1,128]{1,0:T(1,128)S(1)} %get-tuple-element.72), channel_id=1, source_target_pairs={{0,8},{8,16},{16,24},{24,32},{32,40},{40,48},{48,56},{56,64},{64,7... | collective-permute-start | bytes 1544 | tf_op jit(solution)/shard_map/ppermute | solution.py:18
  182.9 2.7 %collective-permute-done.38 = f32[1,128]{1,0:T(1,128)S(1)} collective-permute-done((f32[1,128]{1,0:T(1,128)S(1)}, f32[1,128]{1,0:T(1,128)S(1)}, u32[]{:S(2)}, u32[]{:S(2)}) %collective-permute-start.38) | collective-permute-done | bytes 544 | tf_op jit(solution)/shard_map/ppermute | solution.py:18
  189.1 4.2 %collective-permute-done.40 = f32[42,1]{1,0:T(8,128)S(1)} collective-permute-done((f32[42,1]{1,0:T(8,128)S(1)}, f32[42,1]{1,0:T(8,128)S(1)}, u32[]{:S(2)}, u32[]{:S(2)}) %collective-permute-start.40) | collective-permute-done | bytes 200 | tf_op jit(solution)/shard_map/ppermute | solution.py:18
  195.4 2.4 %collective-permute-start.42 = (f32[3,1,40,128]{3,2,1,0:T(8,128)S(1)}, f32[3,1,40,128]{3,2,1,0:T(8,128)S(1)}, u32[]{:S(2)}, u32[]{:S(2)}) collective-permute-start(f32[3,1,40,128]{3,2,1,0:T(8,128)S(1)} %get-tuple-element.42), channel_id=1, source_target_pairs={{0,1},{1,2},{2,3},{3,4},{4,5},{5,6},{6,7},{8,9},{9,10},{10,11},{11... | collective-permute-start | bytes 184328 | tf_op jit(solution)/shard_map/ppermute | solution.py:18
  197.9 3.1 %collective-permute-done.42 = f32[3,1,40,128]{3,2,1,0:T(8,128)S(1)} collective-permute-done((f32[3,1,40,128]{3,2,1,0:T(8,128)S(1)}, f32[3,1,40,128]{3,2,1,0:T(8,128)S(1)}, u32[]{:S(2)}, u32[]{:S(2)}) %collective-permute-start.42) | collective-permute-done | bytes 61472 | tf_op jit(solution)/shard_map/ppermute | solution.py:18
  202.9 3.9 %collective-permute-start.44 = (f32[3,18,1,128]{3,2,1,0:T(1,128)S(1)}, f32[3,18,1,128]{3,2,1,0:T(1,128)S(1)}, u32[]{:S(2)}, u32[]{:S(2)}) collective-permute-start(f32[3,18,1,128]{3,2,1,0:T(1,128)S(1)} %get-tuple-element.40), channel_id=1, source_target_pairs={{0,8},{8,16},{16,24},{24,32},{32,40},{40,48},{48,56},{56,64},{64,7... | collective-permute-start | bytes 82952 | tf_op jit(solution)/shard_map/ppermute | solution.py:18
  206.9 3.0 %collective-permute-done.44 = f32[3,18,1,128]{3,2,1,0:T(1,128)S(1)} collective-permute-done((f32[3,18,1,128]{3,2,1,0:T(1,128)S(1)}, f32[3,18,1,128]{3,2,1,0:T(1,128)S(1)}, u32[]{:S(2)}, u32[]{:S(2)}) %collective-permute-start.44) | collective-permute-done | bytes 27680 | tf_op jit(solution)/shard_map/ppermute | solution.py:18
  213.8 1.9 collective-permute-start.45
  220.8 2.6 %collective-permute-done.46 = f32[3,18,42,1]{2,3,1,0:T(1,128)S(1)} collective-permute-done((f32[3,18,42,1]{2,3,1,0:T(1,128)S(1)}, f32[3,18,42,1]{2,3,1,0:T(1,128)S(1)}, u32[]{:S(2)}, u32[]{:S(2)}) %collective-permute-start.46) | collective-permute-done | bytes 9104 | tf_op jit(solution)/shard_map/ppermute | solution.py:18
  225.1 4.2 %fusion.2 = f32[3,16,40,128]{3,2,1,0:T(8,128)S(1)} fusion(f32[3,16,40,128]{3,2,1,0:T(8,128)S(1)} %add_dynamic-update-slice_fusion, f32[3,18,42,1]{3,2,1,0:T(8,128)} %copy.269, f32[3,18,1,128]{3,2,1,0:T(1,128)S(1)} %collective-permute-done.43, f32[3,18,1,128]{3,2,1,0:T(1,128)S(1)} %collective-permute-done.44, ...), kind=kLoop, calls=%fused_computation.22 | loop fusion | flops 8601600 | bytes 4128480 | tf_op jit(solution)/shard_map/add | solution.py:56
  (229 shorter events, 71.9 us)
Async XLA Ops:
  2.6 6.0 %collective-permute-start = (f32[4,1,40,128]{3,2,1,0:T(8,128)S(1)}, f32[4,1,40,128]{3,2,1,0:T(8,128)S(1)}, u32[]{:S(2)}, u32[]{:S(2)}) collective-permute-start(f32[4,1,40,128]{3,2,1,0:T(8,128)S(1)} %get-tuple-element.38), channel_id=1, source_target_pairs={{0,1},{1,2},{2,3},{3,4},{4,5},{5,6},{6,7},{8,9},{9,10},{10,11},{11... | collective-permute-start | bytes 245768 | tf_op jit(solution)/shard_map/ppermute | solution.py:18
  4.5 5.7 %collective-permute-start.1 = (f32[4,1,40,128]{3,2,1,0:T(8,128)S(1)}, f32[4,1,40,128]{3,2,1,0:T(8,128)S(1)}, u32[]{:S(2)}, u32[]{:S(2)}) collective-permute-start(f32[4,1,40,128]{3,2,1,0:T(8,128)S(1)} %get-tuple-element.39), channel_id=1, source_target_pairs={{1,0},{2,1},{3,2},{4,3},{5,4},{6,5},{7,6},{9,8},{10,9},{11,10},{12... | collective-permute-start | bytes 245768 | tf_op jit(solution)/shard_map/ppermute | solution.py:20
  10.3 7.3 %collective-permute-start.2 = (f32[4,18,1,128]{3,0,2,1:T(4,128)S(1)}, f32[4,18,1,128]{3,0,2,1:T(4,128)S(1)}, u32[]{:S(2)}, u32[]{:S(2)}) collective-permute-start(f32[4,18,1,128]{3,0,2,1:T(4,128)S(1)} %copy.276), channel_id=1, source_target_pairs={{0,8},{8,16},{16,24},{24,32},{32,40},{40,48},{48,56},{56,64},{64,7... | collective-permute-start | bytes 110600 | tf_op jit(solution)/shard_map/ppermute | solution.py:18
  13.2 5.9 %collective-permute-start.3 = (f32[4,18,1,128]{3,0,2,1:T(4,128)S(1)}, f32[4,18,1,128]{3,0,2,1:T(4,128)S(1)}, u32[]{:S(2)}, u32[]{:S(2)}) collective-permute-start(f32[4,18,1,128]{3,0,2,1:T(4,128)S(1)} %copy.277), channel_id=1, source_target_pairs={{8,0},{16,8},{24,16},{32,24},{40,32},{48,40},{56,48},{64,56},{72,6... | collective-permute-start | bytes 110600 | tf_op jit(solution)/shard_map/ppermute | solution.py:20
  23.3 7.2 %collective-permute-start.4 = (f32[4,18,42,1]{2,0,3,1:T(4,128)S(1)}, f32[4,18,42,1]{2,0,3,1:T(4,128)S(1)}, u32[]{:S(2)}, u32[]{:S(2)}) collective-permute-start(f32[4,18,42,1]{2,0,3,1:T(4,128)S(1)} %copy.246), channel_id=1, source_target_pairs={{0,128},{128,256},{256,384},{1,129},{129,257},{257,385},{2,130},{1... | collective-permute-start | bytes 36296 | tf_op jit(solution)/shard_map/ppermute | solution.py:18
  25.3 6.2 %collective-permute-start.5 = (f32[4,18,42,1]{2,0,3,1:T(4,128)S(1)}, f32[4,18,42,1]{2,0,3,1:T(4,128)S(1)}, u32[]{:S(2)}, u32[]{:S(2)}) collective-permute-start(f32[4,18,42,1]{2,0,3,1:T(4,128)S(1)} %copy.247), channel_id=1, source_target_pairs={{128,0},{256,128},{384,256},{129,1},{257,129},{385,257},{130,2},{2... | collective-permute-start | bytes 36296 | tf_op jit(solution)/shard_map/ppermute | solution.py:20
  43.2 3.2 %collective-permute-start.6 = (f32[6,40,128]{2,1,0:T(8,128)S(1)}, f32[6,40,128]{2,1,0:T(8,128)S(1)}, u32[]{:S(2)}, u32[]{:S(2)}) collective-permute-start(f32[6,40,128]{2,1,0:T(8,128)S(1)} %constant_dynamic-update-slice_fusion), channel_id=1, source_target_pairs={{0,1},{1,0},{2,3},{3,2},{4,5},{5,4},{6,7},{7,6},{8,9},{9,8},{10,11... | collective-permute-start | bytes 368648 | tf_op jit(solution)/shard_map/ppermute | solution.py:135
  46.5 10.5 %collective-permute-start.7 = (f32[6,40,128]{2,1,0:T(8,128)S(1)}, f32[6,40,128]{2,1,0:T(8,128)S(1)}, u32[]{:S(2)}, u32[]{:S(2)}) collective-permute-start(f32[6,40,128]{2,1,0:T(8,128)S(1)} %add.410), channel_id=1, source_target_pairs={{0,2},{1,3},{2,0},{3,1},{4,6},{5,7},{6,4},{7,5},{8,10},{9,11},{10,... | collective-permute-start | bytes 368648 | tf_op jit(solution)/shard_map/ppermute | solution.py:135
  48.4 7.3 %collective-permute-start.10 = (f32[1,128]{1,0:T(1,128)S(1)}, f32[1,128]{1,0:T(1,128)S(1)}, u32[]{:S(2)}, u32[]{:S(2)}) collective-permute-start(f32[1,128]{1,0:T(1,128)S(1)} %broadcast.56), channel_id=1, source_target_pairs={{0,8},{8,16},{16,24},{24,32},{32,40},{40,48},{48,56},{56,64},{64,7... | collective-permute-start | bytes 1544 | tf_op jit(solution)/shard_map/ppermute | solution.py:18
  51.3 5.6 %collective-permute-start.9 = (f32[1,128]{1,0:T(1,128)S(1)}, f32[1,128]{1,0:T(1,128)S(1)}, u32[]{:S(2)}, u32[]{:S(2)}) collective-permute-start(f32[1,128]{1,0:T(1,128)S(1)} %broadcast.56), channel_id=1, source_target_pairs={{8,0},{16,8},{24,16},{32,24},{40,32},{48,40},{56,48},{64,56},{72,6... | collective-permute-start | bytes 1544 | tf_op jit(solution)/shard_map/ppermute | solution.py:20
  57.0 10.7 %collective-permute-start.8 = (f32[6,40,128]{2,1,0:T(8,128)S(1)}, f32[6,40,128]{2,1,0:T(8,128)S(1)}, u32[]{:S(2)}, u32[]{:S(2)}) collective-permute-start(f32[6,40,128]{2,1,0:T(8,128)S(1)} %add.411), channel_id=1, source_target_pairs={{0,4},{1,5},{2,6},{3,7},{4,0},{5,1},{6,2},{7,3},{8,12},{9,13},{10,... | collective-permute-start | bytes 368648 | tf_op jit(solution)/shard_map/ppermute | solution.py:135
  62.2 5.7 %collective-permute-start.11 = (f32[42,1]{1,0:T(8,128)S(1)}, f32[42,1]{1,0:T(8,128)S(1)}, u32[]{:S(2)}, u32[]{:S(2)}) collective-permute-start(f32[42,1]{1,0:T(8,128)S(1)} %get-tuple-element.70), channel_id=1, source_target_pairs={{128,0},{256,128},{384,256},{129,1},{257,129},{385,257},{130,2},{2... | collective-permute-start | bytes 512 | tf_op jit(solution)/shard_map/ppermute | solution.py:20
  66.4 5.7 %collective-permute-start.12 = (f32[42,1]{1,0:T(8,128)S(1)}, f32[42,1]{1,0:T(8,128)S(1)}, u32[]{:S(2)}, u32[]{:S(2)}) collective-permute-start(f32[42,1]{1,0:T(8,128)S(1)} %get-tuple-element.71), channel_id=1, source_target_pairs={{0,128},{128,256},{256,384},{1,129},{129,257},{257,385},{2,130},{1... | collective-permute-start | bytes 512 | tf_op jit(solution)/shard_map/ppermute | solution.py:18
  72.2 7.3 %collective-permute-start.13 = (f32[1,128]{1,0:T(1,128)S(1)}, f32[1,128]{1,0:T(1,128)S(1)}, u32[]{:S(2)}, u32[]{:S(2)}) collective-permute-start(f32[1,128]{1,0:T(1,128)S(1)} %get-tuple-element.85), channel_id=1, source_target_pairs={{8,0},{16,8},{24,16},{32,24},{40,32},{48,40},{56,48},{64,56},{72,6... | collective-permute-start | bytes 1544 | tf_op jit(solution)/shard_map/ppermute | solution.py:20
  77.6 6.6 %collective-permute-start.14 = (f32[1,128]{1,0:T(1,128)S(1)}, f32[1,128]{1,0:T(1,128)S(1)}, u32[]{:S(2)}, u32[]{:S(2)}) collective-permute-start(f32[1,128]{1,0:T(1,128)S(1)} %get-tuple-element.84), channel_id=1, source_target_pairs={{0,8},{8,16},{16,24},{24,32},{32,40},{40,48},{48,56},{56,64},{64,7... | collective-permute-start | bytes 1544 | tf_op jit(solution)/shard_map/ppermute | solution.py:18
  84.3 4.2 %collective-permute-start.15 = (f32[42,1]{1,0:T(8,128)S(1)}, f32[42,1]{1,0:T(8,128)S(1)}, u32[]{:S(2)}, u32[]{:S(2)}) collective-permute-start(f32[42,1]{1,0:T(8,128)S(1)} %get-tuple-element.68), channel_id=1, source_target_pairs={{128,0},{256,128},{384,256},{129,1},{257,129},{385,257},{130,2},{2... | collective-permute-start | bytes 512 | tf_op jit(solution)/shard_map/ppermute | solution.py:20
  87.0 5.7 %collective-permute-start.16 = (f32[42,1]{1,0:T(8,128)S(1)}, f32[42,1]{1,0:T(8,128)S(1)}, u32[]{:S(2)}, u32[]{:S(2)}) collective-permute-start(f32[42,1]{1,0:T(8,128)S(1)} %get-tuple-element.69), channel_id=1, source_target_pairs={{0,128},{128,256},{256,384},{1,129},{129,257},{257,385},{2,130},{1... | collective-permute-start | bytes 512 | tf_op jit(solution)/shard_map/ppermute | solution.py:18
  92.8 5.9 %collective-permute-start.17 = (f32[1,128]{1,0:T(1,128)S(1)}, f32[1,128]{1,0:T(1,128)S(1)}, u32[]{:S(2)}, u32[]{:S(2)}) collective-permute-start(f32[1,128]{1,0:T(1,128)S(1)} %get-tuple-element.83), channel_id=1, source_target_pairs={{8,0},{16,8},{24,16},{32,24},{40,32},{48,40},{56,48},{64,56},{72,6... | collective-permute-start | bytes 1544 | tf_op jit(solution)/shard_map/ppermute | solution.py:20
  94.8 6.6 %collective-permute-start.18 = (f32[1,128]{1,0:T(1,128)S(1)}, f32[1,128]{1,0:T(1,128)S(1)}, u32[]{:S(2)}, u32[]{:S(2)}) collective-permute-start(f32[1,128]{1,0:T(1,128)S(1)} %get-tuple-element.82), channel_id=1, source_target_pairs={{0,8},{8,16},{16,24},{24,32},{32,40},{40,48},{48,56},{56,64},{64,7... | collective-permute-start | bytes 1544 | tf_op jit(solution)/shard_map/ppermute | solution.py:18
  101.5 3.9 %collective-permute-start.19 = (f32[42,1]{1,0:T(8,128)S(1)}, f32[42,1]{1,0:T(8,128)S(1)}, u32[]{:S(2)}, u32[]{:S(2)}) collective-permute-start(f32[42,1]{1,0:T(8,128)S(1)} %get-tuple-element.66), channel_id=1, source_target_pairs={{128,0},{256,128},{384,256},{129,1},{257,129},{385,257},{130,2},{2... | collective-permute-start | bytes 512 | tf_op jit(solution)/shard_map/ppermute | solution.py:20
  103.8 5.7 %collective-permute-start.20 = (f32[42,1]{1,0:T(8,128)S(1)}, f32[42,1]{1,0:T(8,128)S(1)}, u32[]{:S(2)}, u32[]{:S(2)}) collective-permute-start(f32[42,1]{1,0:T(8,128)S(1)} %get-tuple-element.67), channel_id=1, source_target_pairs={{0,128},{128,256},{256,384},{1,129},{129,257},{257,385},{2,130},{1... | collective-permute-start | bytes 512 | tf_op jit(solution)/shard_map/ppermute | solution.py:18
  109.7 5.9 %collective-permute-start.21 = (f32[1,128]{1,0:T(1,128)S(1)}, f32[1,128]{1,0:T(1,128)S(1)}, u32[]{:S(2)}, u32[]{:S(2)}) collective-permute-start(f32[1,128]{1,0:T(1,128)S(1)} %get-tuple-element.81), channel_id=1, source_target_pairs={{8,0},{16,8},{24,16},{32,24},{40,32},{48,40},{56,48},{64,56},{72,6... | collective-permute-start | bytes 1544 | tf_op jit(solution)/shard_map/ppermute | solution.py:20
  111.6 6.6 %collective-permute-start.22 = (f32[1,128]{1,0:T(1,128)S(1)}, f32[1,128]{1,0:T(1,128)S(1)}, u32[]{:S(2)}, u32[]{:S(2)}) collective-permute-start(f32[1,128]{1,0:T(1,128)S(1)} %get-tuple-element.80), channel_id=1, source_target_pairs={{0,8},{8,16},{16,24},{24,32},{32,40},{40,48},{48,56},{56,64},{64,7... | collective-permute-start | bytes 1544 | tf_op jit(solution)/shard_map/ppermute | solution.py:18
  118.3 3.4 %collective-permute-start.23 = (f32[42,1]{1,0:T(8,128)S(1)}, f32[42,1]{1,0:T(8,128)S(1)}, u32[]{:S(2)}, u32[]{:S(2)}) collective-permute-start(f32[42,1]{1,0:T(8,128)S(1)} %get-tuple-element.64), channel_id=1, source_target_pairs={{128,0},{256,128},{384,256},{129,1},{257,129},{385,257},{130,2},{2... | collective-permute-start | bytes 512 | tf_op jit(solution)/shard_map/ppermute | solution.py:20
  120.3 5.7 %collective-permute-start.24 = (f32[42,1]{1,0:T(8,128)S(1)}, f32[42,1]{1,0:T(8,128)S(1)}, u32[]{:S(2)}, u32[]{:S(2)}) collective-permute-start(f32[42,1]{1,0:T(8,128)S(1)} %get-tuple-element.65), channel_id=1, source_target_pairs={{0,128},{128,256},{256,384},{1,129},{129,257},{257,385},{2,130},{1... | collective-permute-start | bytes 512 | tf_op jit(solution)/shard_map/ppermute | solution.py:18
  126.1 67.3 %copy-start.1 = (f32[3,16,40,128]{3,2,1,0:T(8,128)S(1)}, f32[3,16,40,128]{3,2,1,0:T(8,128)}, u32[]{:S(2)}) copy-start(f32[3,16,40,128]{3,2,1,0:T(8,128)} %param.9) | copy-start | bytes 2949124
  126.1 6.0 %collective-permute-start.25 = (f32[1,128]{1,0:T(1,128)S(1)}, f32[1,128]{1,0:T(1,128)S(1)}, u32[]{:S(2)}, u32[]{:S(2)}) collective-permute-start(f32[1,128]{1,0:T(1,128)S(1)} %get-tuple-element.79), channel_id=1, source_target_pairs={{8,0},{16,8},{24,16},{32,24},{40,32},{48,40},{56,48},{64,56},{72,6... | collective-permute-start | bytes 1544 | tf_op jit(solution)/shard_map/ppermute | solution.py:20
  128.9 6.6 %collective-permute-start.26 = (f32[1,128]{1,0:T(1,128)S(1)}, f32[1,128]{1,0:T(1,128)S(1)}, u32[]{:S(2)}, u32[]{:S(2)}) collective-permute-start(f32[1,128]{1,0:T(1,128)S(1)} %get-tuple-element.78), channel_id=1, source_target_pairs={{0,8},{8,16},{16,24},{24,32},{32,40},{40,48},{48,56},{56,64},{64,7... | collective-permute-start | bytes 1544 | tf_op jit(solution)/shard_map/ppermute | solution.py:18
  135.7 3.4 %collective-permute-start.27 = (f32[42,1]{1,0:T(8,128)S(1)}, f32[42,1]{1,0:T(8,128)S(1)}, u32[]{:S(2)}, u32[]{:S(2)}) collective-permute-start(f32[42,1]{1,0:T(8,128)S(1)} %get-tuple-element.62), channel_id=1, source_target_pairs={{128,0},{256,128},{384,256},{129,1},{257,129},{385,257},{130,2},{2... | collective-permute-start | bytes 512 | tf_op jit(solution)/shard_map/ppermute | solution.py:20
  137.6 5.7 %collective-permute-start.28 = (f32[42,1]{1,0:T(8,128)S(1)}, f32[42,1]{1,0:T(8,128)S(1)}, u32[]{:S(2)}, u32[]{:S(2)}) collective-permute-start(f32[42,1]{1,0:T(8,128)S(1)} %get-tuple-element.63), channel_id=1, source_target_pairs={{0,128},{128,256},{256,384},{1,129},{129,257},{257,385},{2,130},{1... | collective-permute-start | bytes 512 | tf_op jit(solution)/shard_map/ppermute | solution.py:18
  143.4 5.9 %collective-permute-start.29 = (f32[1,128]{1,0:T(1,128)S(1)}, f32[1,128]{1,0:T(1,128)S(1)}, u32[]{:S(2)}, u32[]{:S(2)}) collective-permute-start(f32[1,128]{1,0:T(1,128)S(1)} %get-tuple-element.77), channel_id=1, source_target_pairs={{8,0},{16,8},{24,16},{32,24},{40,32},{48,40},{56,48},{64,56},{72,6... | collective-permute-start | bytes 1544 | tf_op jit(solution)/shard_map/ppermute | solution.py:20
  146.1 6.6 %collective-permute-start.30 = (f32[1,128]{1,0:T(1,128)S(1)}, f32[1,128]{1,0:T(1,128)S(1)}, u32[]{:S(2)}, u32[]{:S(2)}) collective-permute-start(f32[1,128]{1,0:T(1,128)S(1)} %get-tuple-element.76), channel_id=1, source_target_pairs={{0,8},{8,16},{16,24},{24,32},{32,40},{40,48},{48,56},{56,64},{64,7... | collective-permute-start | bytes 1544 | tf_op jit(solution)/shard_map/ppermute | solution.py:18
  152.9 3.4 %collective-permute-start.31 = (f32[42,1]{1,0:T(8,128)S(1)}, f32[42,1]{1,0:T(8,128)S(1)}, u32[]{:S(2)}, u32[]{:S(2)}) collective-permute-start(f32[42,1]{1,0:T(8,128)S(1)} %get-tuple-element.60), channel_id=1, source_target_pairs={{128,0},{256,128},{384,256},{129,1},{257,129},{385,257},{130,2},{2... | collective-permute-start | bytes 512 | tf_op jit(solution)/shard_map/ppermute | solution.py:20
  154.8 5.7 %collective-permute-start.32 = (f32[42,1]{1,0:T(8,128)S(1)}, f32[42,1]{1,0:T(8,128)S(1)}, u32[]{:S(2)}, u32[]{:S(2)}) collective-permute-start(f32[42,1]{1,0:T(8,128)S(1)} %get-tuple-element.61), channel_id=1, source_target_pairs={{0,128},{128,256},{256,384},{1,129},{129,257},{257,385},{2,130},{1... | collective-permute-start | bytes 512 | tf_op jit(solution)/shard_map/ppermute | solution.py:18
  160.6 5.9 %collective-permute-start.33 = (f32[1,128]{1,0:T(1,128)S(1)}, f32[1,128]{1,0:T(1,128)S(1)}, u32[]{:S(2)}, u32[]{:S(2)}) collective-permute-start(f32[1,128]{1,0:T(1,128)S(1)} %get-tuple-element.75), channel_id=1, source_target_pairs={{8,0},{16,8},{24,16},{32,24},{40,32},{48,40},{56,48},{64,56},{72,6... | collective-permute-start | bytes 1544 | tf_op jit(solution)/shard_map/ppermute | solution.py:20
  162.5 6.6 %collective-permute-start.34 = (f32[1,128]{1,0:T(1,128)S(1)}, f32[1,128]{1,0:T(1,128)S(1)}, u32[]{:S(2)}, u32[]{:S(2)}) collective-permute-start(f32[1,128]{1,0:T(1,128)S(1)} %get-tuple-element.74), channel_id=1, source_target_pairs={{0,8},{8,16},{16,24},{24,32},{32,40},{40,48},{48,56},{56,64},{64,7... | collective-permute-start | bytes 1544 | tf_op jit(solution)/shard_map/ppermute | solution.py:18
  169.3 3.4 %collective-permute-start.35 = (f32[42,1]{1,0:T(8,128)S(1)}, f32[42,1]{1,0:T(8,128)S(1)}, u32[]{:S(2)}, u32[]{:S(2)}) collective-permute-start(f32[42,1]{1,0:T(8,128)S(1)} %get-tuple-element.58), channel_id=1, source_target_pairs={{128,0},{256,128},{384,256},{129,1},{257,129},{385,257},{130,2},{2... | collective-permute-start | bytes 512 | tf_op jit(solution)/shard_map/ppermute | solution.py:20
  171.2 5.7 %collective-permute-start.36 = (f32[42,1]{1,0:T(8,128)S(1)}, f32[42,1]{1,0:T(8,128)S(1)}, u32[]{:S(2)}, u32[]{:S(2)}) collective-permute-start(f32[42,1]{1,0:T(8,128)S(1)} %get-tuple-element.59), channel_id=1, source_target_pairs={{0,128},{128,256},{256,384},{1,129},{129,257},{257,385},{2,130},{1... | collective-permute-start | bytes 512 | tf_op jit(solution)/shard_map/ppermute | solution.py:18
  177.0 5.9 %collective-permute-start.37 = (f32[1,128]{1,0:T(1,128)S(1)}, f32[1,128]{1,0:T(1,128)S(1)}, u32[]{:S(2)}, u32[]{:S(2)}) collective-permute-start(f32[1,128]{1,0:T(1,128)S(1)} %get-tuple-element.73), channel_id=1, source_target_pairs={{8,0},{16,8},{24,16},{32,24},{40,32},{48,40},{56,48},{64,56},{72,6... | collective-permute-start | bytes 1544 | tf_op jit(solution)/shard_map/ppermute | solution.py:20
  178.9 6.6 %collective-permute-start.38 = (f32[1,128]{1,0:T(1,128)S(1)}, f32[1,128]{1,0:T(1,128)S(1)}, u32[]{:S(2)}, u32[]{:S(2)}) collective-permute-start(f32[1,128]{1,0:T(1,128)S(1)} %get-tuple-element.72), channel_id=1, source_target_pairs={{0,8},{8,16},{16,24},{24,32},{32,40},{40,48},{48,56},{56,64},{64,7... | collective-permute-start | bytes 1544 | tf_op jit(solution)/shard_map/ppermute | solution.py:18
  185.7 3.4 %collective-permute-start.39 = (f32[42,1]{1,0:T(8,128)S(1)}, f32[42,1]{1,0:T(8,128)S(1)}, u32[]{:S(2)}, u32[]{:S(2)}) collective-permute-start(f32[42,1]{1,0:T(8,128)S(1)} %get-tuple-element.56), channel_id=1, source_target_pairs={{128,0},{256,128},{384,256},{129,1},{257,129},{385,257},{130,2},{2... | collective-permute-start | bytes 512 | tf_op jit(solution)/shard_map/ppermute | solution.py:20
  187.6 5.7 %collective-permute-start.40 = (f32[42,1]{1,0:T(8,128)S(1)}, f32[42,1]{1,0:T(8,128)S(1)}, u32[]{:S(2)}, u32[]{:S(2)}) collective-permute-start(f32[42,1]{1,0:T(8,128)S(1)} %get-tuple-element.57), channel_id=1, source_target_pairs={{0,128},{128,256},{256,384},{1,129},{129,257},{257,385},{2,130},{1... | collective-permute-start | bytes 512 | tf_op jit(solution)/shard_map/ppermute | solution.py:18
  193.5 4.3 %collective-permute-start.41 = (f32[3,1,40,128]{3,2,1,0:T(8,128)S(1)}, f32[3,1,40,128]{3,2,1,0:T(8,128)S(1)}, u32[]{:S(2)}, u32[]{:S(2)}) collective-permute-start(f32[3,1,40,128]{3,2,1,0:T(8,128)S(1)} %get-tuple-element.43), channel_id=1, source_target_pairs={{1,0},{2,1},{3,2},{4,3},{5,4},{6,5},{7,6},{9,8},{10,9},{11,10},{12... | collective-permute-start | bytes 184328 | tf_op jit(solution)/shard_map/ppermute | solution.py:20
  195.4 5.5 %collective-permute-start.42 = (f32[3,1,40,128]{3,2,1,0:T(8,128)S(1)}, f32[3,1,40,128]{3,2,1,0:T(8,128)S(1)}, u32[]{:S(2)}, u32[]{:S(2)}) collective-permute-start(f32[3,1,40,128]{3,2,1,0:T(8,128)S(1)} %get-tuple-element.42), channel_id=1, source_target_pairs={{0,1},{1,2},{2,3},{3,4},{4,5},{5,6},{6,7},{8,9},{9,10},{10,11},{11... | collective-permute-start | bytes 184328 | tf_op jit(solution)/shard_map/ppermute | solution.py:18
  201.0 5.9 %collective-permute-start.43 = (f32[3,18,1,128]{3,2,1,0:T(1,128)S(1)}, f32[3,18,1,128]{3,2,1,0:T(1,128)S(1)}, u32[]{:S(2)}, u32[]{:S(2)}) collective-permute-start(f32[3,18,1,128]{3,2,1,0:T(1,128)S(1)} %get-tuple-element.41), channel_id=1, source_target_pairs={{8,0},{16,8},{24,16},{32,24},{40,32},{48,40},{56,48},{64,56},{72,6... | collective-permute-start | bytes 82952 | tf_op jit(solution)/shard_map/ppermute | solution.py:20
  202.9 7.0 %collective-permute-start.44 = (f32[3,18,1,128]{3,2,1,0:T(1,128)S(1)}, f32[3,18,1,128]{3,2,1,0:T(1,128)S(1)}, u32[]{:S(2)}, u32[]{:S(2)}) collective-permute-start(f32[3,18,1,128]{3,2,1,0:T(1,128)S(1)} %get-tuple-element.40), channel_id=1, source_target_pairs={{0,8},{8,16},{16,24},{24,32},{32,40},{40,48},{48,56},{56,64},{64,7... | collective-permute-start | bytes 82952 | tf_op jit(solution)/shard_map/ppermute | solution.py:18
  213.8 5.4 %collective-permute-start.45 = (f32[3,18,42,1]{2,3,1,0:T(1,128)S(1)}, f32[3,18,42,1]{2,3,1,0:T(1,128)S(1)}, u32[]{:S(2)}, u32[]{:S(2)}) collective-permute-start(f32[3,18,42,1]{2,3,1,0:T(1,128)S(1)} %copy.278), channel_id=1, source_target_pairs={{128,0},{256,128},{384,256},{129,1},{257,129},{385,257},{130,2},{2... | collective-permute-start | bytes 27224 | tf_op jit(solution)/shard_map/ppermute | solution.py:20
  217.7 5.8 %collective-permute-start.46 = (f32[3,18,42,1]{2,3,1,0:T(1,128)S(1)}, f32[3,18,42,1]{2,3,1,0:T(1,128)S(1)}, u32[]{:S(2)}, u32[]{:S(2)}) collective-permute-start(f32[3,18,42,1]{2,3,1,0:T(1,128)S(1)} %copy.279), channel_id=1, source_target_pairs={{0,128},{128,256},{256,384},{1,129},{129,257},{257,385},{2,130},{1... | collective-permute-start | bytes 27224 | tf_op jit(solution)/shard_map/ppermute | solution.py:18
  (41 other events, 168.6 us)
